TPU v7x, 32 devices: a whole 2x2x4 slice. The times are simulated.
32 devices in a mesh: section: 2 (over core), dp: 16 (over z, y, x).
Axes of the slice: x: 2, y: 2, z: 4, core: 2. Of those that a mesh axis runs over, the one named last changes fastest.
Arguments:
- tokens: bfloat16 [4, 8192, 768], P(None, 'dp'), may hold values from -9 to 9
- valid: int32 [4, 8192], P(None, 'dp'), may hold values from 0 to 1, as said below
- cotangent: bfloat16 [4, 8192, 768], P(None, 'dp'), may hold values from -11 to 11
- qkv_weight: bfloat16 [2, 768, 2304], P('section'), may hold values from -0.21875 to 0.21875
- out_weight: bfloat16 [2, 768, 768], P('section'), may hold values from -0.875 to 0.875
- ffn_in: bfloat16 [2, 768, 3072], P('section'), may hold values from -0.21875 to 0.21875
- ffn_out: bfloat16 [2, 3072, 768], P('section'), may hold values from -0.15625 to 0.15625
- attn_down: bfloat16 [2, 768, 64], P('section'), may hold values from -0.21875 to 0.21875
- attn_down_bias: float32 [2, 64], P('section'), may hold values from -3 to 3
- attn_up: bfloat16 [2, 64, 768], P('section'), may hold values from -0.75 to 0.75
- attn_up_bias: float32 [2, 768], P('section'), may hold values from -2 to 2
- norm1_gain: float32 [2, 768], P('section'), may hold values from 0.5 to 1.5
- norm1_bias: float32 [2, 768], P('section'), may hold values from -1 to 1
- ffn_down: bfloat16 [2, 768, 64], P('section'), may hold values from -0.21875 to 0.21875
- ffn_down_bias: float32 [2, 64], P('section'), may hold values from -3 to 3
- ffn_up: bfloat16 [2, 64, 768], P('section'), may hold values from -0.75 to 0.75
- ffn_up_bias: float32 [2, 768], P('section'), may hold values from -2 to 2
- norm2_gain: float32 [2, 768], P('section'), may hold values from 0.5 to 1.5
- norm2_bias: float32 [2, 768], P('section'), may hold values from -1 to 1
Outputs:
- result: bfloat16 [4, 8192, 768], P(None, 'dp')
- input_grad: bfloat16 [4, 8192, 768], P('section', 'dp')
- grad_attn_down: float32 [2, 768, 64], P('section')
- grad_attn_down_bias: float32 [2, 64], P('section')
- grad_attn_up: float32 [2, 64, 768], P('section')
- grad_attn_up_bias: float32 [2, 768], P('section')
- grad_norm1_gain: float32 [2, 768], P('section')
- grad_norm1_bias: float32 [2, 768], P('section')
- grad_ffn_down: float32 [2, 768, 64], P('section')
- grad_ffn_down_bias: float32 [2, 64], P('section')
- grad_ffn_up: float32 [2, 64, 768], P('section')
- grad_ffn_up_bias: float32 [2, 768], P('section')
- grad_norm2_gain: float32 [2, 768], P('section')
- grad_norm2_bias: float32 [2, 768], P('section')
- rms_values: float32 [2, 3], P('section')
Inputs may be any that keep to these rules, and one draw needn't show every extreme that they name: `valid`: in micro-batch m the slots form sequences of 64 * 2**m consecutive slots; in each sequence the ones are a leading run of at least one slot.
All inputs are finite; a program needn't handle non-finite values.
Results may differ from a plain program's by a relative error of at most 0.034.
Values may be sent and summed in bfloat16 or wider, within the bound.
No kernel may reach another device: no remote copies, remote signals or barrier semaphores. Data moves between devices by JAX's collectives and lax.ppermute only.
A program may use at most 320 MiB of HBM per device.

v0:
```python
import math
from types import SimpleNamespace
from typing import Any, NamedTuple

import jax
import jax.numpy as jnp
from jax import lax
from jax.experimental import pallas as pl
from jax.experimental.pallas import tpu as pltpu
from jax.sharding import PartitionSpec as P

NEGATIVE = -1e30
EPSILON = 1e-12
ROOT_HALF = 0.7071067811865476
INV_ROOT_TAU = 0.3989422804014327
LOG2E = 1.4426950408889634

PLAN = ((0, 1), (3, 2))

BF = jnp.bfloat16
F32 = jnp.float32
ANY = pl.BlockSpec(memory_space=pl.ANY)
VMEM_LIMIT = 60 << 20

ATTN_DOWN, ATTN_UP, FFN_DOWN, FFN_UP = range(4)
MATRIX_ROWS, BLOCK_ROWS = 64, 72
UP_BIAS, GAIN, BIAS, DOWN_BIAS = range(64, 68)
STATS = 64


class Layer(NamedTuple):
    qkv: Any
    out: Any
    win: Any
    wout: Any
    mats: Any
    vecs: Any


class Adapter(NamedTuple):
    down: Any
    down_bias: Any
    up: Any
    up_bias: Any
    gain: Any
    bias: Any


def mm(a, b):
    return jnp.dot(a, b, preferred_element_type=F32)


def mm_nt(a, b):
    return lax.dot_general(a, b, (((1,), (1,)), ((), ())), preferred_element_type=F32)


def mm_tn(a, b):
    return lax.dot_general(a, b, (((0,), (0,)), ((), ())), preferred_element_type=F32)


def span_of(index, size, base=0):
    start = index * size + base
    return pl.ds(start if isinstance(index, int) else pl.multiple_of(start, size), size)


def steps(count, body, unroll=None):
    if unroll is None or unroll >= count:
        for at in range(count):
            body(at)
        return

    def some(group, carry):
        for at in range(unroll):
            body(group * unroll + at)
        return carry

    lax.fori_loop(0, count // unroll, some, 0)


PAIRS_FORWARD, PAIRS_BACKWARD = 2, 1
FFN_FORWARD, FFN_BACKWARD = 12, 12


def gelu_both(z):
    cdf = 0.5 + 0.5 * lax.erf(z * ROOT_HALF)
    bell = jnp.exp2(z * z * (-0.5 * LOG2E))
    return z * cdf, cdf + (z * INV_ROOT_TAU) * bell


def nothing(at):
    pass


def qkv_phase(h, qkv, packed, need=nothing):
    width = h.shape[-1]

    def one(at):
        need(at)
        cols = span_of(at, 256)
        y = mm(h[...], qkv[:, cols])
        if at < width // 256:
            y = y * 0.125
        packed[:, cols] = y.astype(BF)

    steps(qkv.shape[1] // 256, one)


def lane_half(shape):
    return lax.broadcasted_iota(jnp.int32, shape, len(shape) - 1) < 64


def split_pair(pair, first):
    zero = jnp.zeros_like(pair)
    return jnp.concatenate([jnp.where(first, pair, zero), jnp.where(first, zero, pair)], axis=0)


def values_and_ones(v2, first):
    one = jnp.ones_like(v2)
    return jnp.concatenate([split_pair(v2, first), split_pair(one, first)], axis=1)


def by_level(level, run):
    @pl.when(level <= 2)
    def _():
        run(256)

    @pl.when(level == 3)
    def _():
        run(512)


def pair_ignored(pair, length):
    pass


def attention_forward(level, valid, bias, packed, context, portions, linv, done=pair_ignored):
    rows, width = context.shape
    query = 256

    def run(length):
        live = valid_row(valid, level)
        barred = jnp.where(live > 0, 0.0, NEGATIVE)
        if length == 256:
            shift = 6 + level
            a = lax.broadcasted_iota(jnp.int32, (256, 256), 0) >> shift
            b = lax.broadcasted_iota(jnp.int32, (256, 256), 1) >> shift
            apart = jnp.where(a == b, 0.0, NEGATIVE)
            for block in range(rows // 256):
                bias[span_of(block, 256), :] = apart + barred[:, block * 256 : (block + 1) * 256]
        first = lane_half((length, 128))

        def pair(at):
            lanes = span_of(at, 128)
            for block in range(rows // length):
                base = block * length
                k2 = packed[base : base + length, span_of(at, 128, width)]
                v2 = packed[base : base + length, span_of(at, 128, 2 * width)]
                kk = split_pair(k2, first)
                vv = values_and_ones(v2, first)
                for part in range(length // query):
                    at_rows = pl.ds(base + part * query, query)
                    scores = mm_nt(packed[at_rows, lanes], kk)
                    halves = []
                    for head in range(2):
                        s = scores[:, head * length : (head + 1) * length]
                        s = s + (bias[at_rows, :] if length == 256 else barred)
                        top = jnp.max(s, axis=-1, keepdims=True)
                        halves.append(jnp.exp2((s - top) * LOG2E).astype(BF))
                    p = jnp.concatenate(halves, axis=1)
                    portions[at, at_rows, 0 : 2 * length] = p
                    both = mm(p, vv)
                    inverse = 1.0 / both[:, 128:]
                    linv[at_rows, lanes] = inverse.astype(BF)
                    context[at_rows, lanes] = (both[:, :128] * inverse).astype(BF)
            done(at, length)

        steps(width // 128, pair, PAIRS_FORWARD)

    by_level(level, run)


def attention_backward(level, packed, context, portions, linv, dcontext, dpacked, slot=0, copy=None):
    rows, width = context.shape
    query = 256

    def run(length):
        first = lane_half((length, 128))

        def pair(at):
            if copy is not None:
                copy(slot, at, length).wait()
            lanes = span_of(at, 128)
            for block in range(rows // length):
                base = block * length
                whole = pl.ds(base, length)
                k2 = packed[whole, span_of(at, 128, width)]
                v2 = packed[whole, span_of(at, 128, 2 * width)]
                kk = split_pair(k2, first)
                vv = values_and_ones(v2, first)
                dk = None
                dv = None
                for part in range(length // query):
                    at_rows = pl.ds(base + part * query, query)
                    out = dcontext[at_rows, lanes].astype(F32) * linv[at_rows, lanes].astype(F32)
                    low = out.astype(BF)
                    both = jnp.concatenate(
                        [low, (-out * context[at_rows, lanes].astype(F32)).astype(BF)], axis=1
                    )
                    p = portions[at, at_rows, 0 : 2 * length]
                    ds = p * mm_nt(both, vv).astype(BF)
                    q2 = packed[at_rows, lanes]
                    dpacked[at_rows, lanes] = (mm(ds, kk) * 0.125).astype(BF)
                    more_k = mm_tn(ds, q2)
                    more_v = mm_tn(p, low)
                    dk = more_k if dk is None else dk + more_k
                    dv = more_v if dv is None else dv + more_v
                dk = jnp.where(first, dk[:length], dk[length:])
                dv = jnp.where(first, dv[:length], dv[length:])
                dpacked[whole, span_of(at, 128, width)] = dk.astype(BF)
                dpacked[whole, span_of(at, 128, 2 * width)] = dv.astype(BF)

        steps(width // 128, pair, PAIRS_BACKWARD)

    by_level(level, run)


def project(x, weight, out):
    def one(at):
        cols = span_of(at, 256)
        out[:, cols] = mm(x[...], weight[:, cols]).astype(BF)

    steps(out.shape[1] // 256, one)


def project_back(x, weight, out):
    def one(at):
        cols = span_of(at, 256)
        out[:, cols] = mm_nt(x[...], weight[cols, :]).astype(BF)

    steps(out.shape[1] // 256, one)


def adapter_norm(base, inner, live, w, saved, out, stats):
    act, slope, std, scale = saved
    rows, width = inner.shape
    block = 128

    def one(at):
        r = span_of(at, block)
        x = inner[r, :]
        pre = mm_nt(x, w.down[...]) + w.down_bias
        a, g = gelu_both(pre)
        a = a.astype(BF)
        act[r, :] = a
        slope[r, :] = g
        branch = x.astype(F32) + (mm(a, w.up[...]) + w.up_bias)
        total = base[r, :].astype(F32) + branch
        alive = live[r, :]
        stats[0:1, :] += jnp.sum(branch * branch * alive, axis=0, keepdims=True)
        mean = jnp.mean(total, axis=-1, keepdims=True)
        centered = total - mean
        variance = jnp.mean(centered * centered, axis=-1, keepdims=True)
        square = jnp.sum((variance + mean * mean) * alive, axis=0, keepdims=True)
        stats[1:2, :] += jnp.broadcast_to(square, (1, width))
        s = lax.rsqrt(variance + EPSILON)
        n = centered * s
        std[r, :] = n.astype(BF)
        scale[r, :] = s
        out[r, :] = (n * w.gain + w.bias).astype(BF)

    steps(rows // block, one)


def ffn_forward(middle, win, wout, act, slope, returned, need=nothing):
    need(0)
    expand(middle, win, act, slope)
    need(1)
    project(act, wout, returned)


def expand(middle, win, act, slope):

    def one(at):
        cols = span_of(at, 256)
        z = mm(middle[...], win[:, cols])
        a, g = gelu_both(z)
        act[:, cols] = a.astype(BF)
        slope[:, cols] = g.astype(BF)

    steps(win.shape[1] // 256, one, FFN_FORWARD)


def norm_adapter_back(dtotal, saved, inner, w, low, dpre_all, dinner, grads_down, grads_up):
    act, slope, std, scale = saved
    rows = inner.shape[0]
    block = 128

    def add(row, values):
        grads_down[row : row + 1, 0 : values.shape[1]] += jnp.sum(values, axis=0, keepdims=True)

    def one(at):
        r = span_of(at, block)
        g = dtotal[r, :]
        n = std[r, :].astype(F32)
        add(GAIN, g * n)
        add(BIAS, g)
        gg = g * w.gain
        m1 = jnp.mean(gg, axis=-1, keepdims=True)
        m2 = jnp.mean(gg * n, axis=-1, keepdims=True)
        d = scale[r, :] * (gg - m1 - n * m2)
        dtotal[r, :] = d
        e = d.astype(BF)
        low[r, :] = e
        e32 = e.astype(F32)
        add(UP_BIAS, e32)
        dpre = (mm_nt(e, w.up[...]) * slope[r, :]).astype(BF)
        dpre_all[r, :] = dpre
        add(DOWN_BIAS, dpre.astype(F32))
        dinner[r, :] = (e32 + mm(dpre, w.down[...])).astype(BF)

    steps(rows // block, one)
    grads_up[0:MATRIX_ROWS, :] += mm_tn(act[...], low[...])
    grads_down[0:MATRIX_ROWS, :] += mm_tn(dpre_all[...], inner[...])


def ffn_backward(dreturned, win, wout, slope, dexp, dsecond):
    expand_back(dreturned, wout, slope, dexp)
    project_add(dexp, win, dsecond)


def expand_back(dreturned, wout, slope, dexp):
    def one(at):
        cols = span_of(at, 256)
        d = mm_nt(dreturned[...], wout[cols, :])
        dexp[:, cols] = d.astype(BF) * slope[:, cols]

    steps(wout.shape[0] // 256, one, FFN_BACKWARD)


def project_add(x, weight, out):
    def one(at):
        cols = span_of(at, 256)
        out[:, cols] += mm_nt(x[...], weight[cols, :])

    steps(weight.shape[0] // 256, one)


def input_backward(dpacked, qkv, dfirst, dentry):
    def one(at):
        cols = span_of(at, 256)
        d = mm_nt(dpacked[...], qkv[cols, :])
        dentry[:, cols] = (dfirst[:, cols].astype(F32) + d).astype(BF)

    steps(qkv.shape[0] // 256, one)


class Item(NamedTuple):
    make: Any
    ref: Any

    def start(self):
        self.make().start()

    def wait(self):
        self.make().wait()


class Call:
    def __init__(self, section, slots, base=0):
        self.slots, self.base = slots, base
        self.args, self.in_specs, self.in_names = [], [], []
        self.outs, self.out_specs, self.out_names = [], [], []
        self.scratch, self.scratch_names = [], []
        self.kinds = {}
        self.section = section
        self.flops = 0
        self.limit = VMEM_LIMIT

    def _add(self, name, array, spec):
        self.args.append(array)
        self.in_specs.append(spec)
        self.in_names.append(name)

    def _temp(self, name, shape):
        self.scratch.append(shape)
        self.scratch_names.append(name)

    def whole(self, **arrays):
        for name, array in arrays.items():
            zeros = (0,) * array.ndim
            self._add(name, array, pl.BlockSpec(array.shape, lambda i, s, zeros=zeros: zeros))

    def raw(self, **arrays):
        for name, array in arrays.items():
            self._add(name, array, ANY)

    def load(self, micro=False, depth=2, **arrays):
        for name, array in arrays.items():
            depth_of = min(depth, self.slots)
            self._add((name, 0), array, ANY)
            self._temp((name, 1), pltpu.VMEM((depth_of,) + array.shape[1:], array.dtype))
            self._temp((name, 2), pltpu.SemaphoreType.DMA((depth_of,)))
            self.kinds[name] = (0, depth_of, micro)

    def save(self, depth=2, **shapes):
        for name, (shape, dtype) in shapes.items():
            depth_of = min(depth, self.slots)
            self.outs.append(jax.ShapeDtypeStruct((self.slots,) + shape, dtype))
            self.out_specs.append(ANY)
            self.out_names.append((name, 0))
            self._temp((name, 1), pltpu.VMEM((depth_of,) + shape, dtype))
            self._temp((name, 2), pltpu.SemaphoreType.DMA((depth_of,)))
            self.kinds[name] = (1, depth_of, False)

    def out(self, **shapes):
        for name, (shape, dtype) in shapes.items():
            self.outs.append(jax.ShapeDtypeStruct(shape, dtype))
            self.out_specs.append(ANY)
            self.out_names.append(name)

    def blocks(self, **shapes):
        for name, (shape, dtype) in shapes.items():
            zeros = (0,) * len(shape)
            self.outs.append(jax.ShapeDtypeStruct(shape, dtype))
            self.out_specs.append(pl.BlockSpec(shape, lambda i, s, zeros=zeros: zeros))
            self.out_names.append(name)

    def temp(self, **shapes):
        for name, (shape, dtype) in shapes.items():
            self._temp(name, pltpu.VMEM(shape, dtype))

    def sems(self, **counts):
        for name, count in counts.items():
            self._temp(name, pltpu.SemaphoreType.DMA(count if isinstance(count, tuple) else (count,)))

    def run(self, body, name):
        names = self.in_names + self.out_names + self.scratch_names
        slots, base = self.slots, self.base

        def kernel(section, *refs):
            step = pl.program_id(0) if slots > 1 else 0
            ref = dict(zip(names, refs))
            r = SimpleNamespace(**{n: v for n, v in ref.items() if isinstance(n, str)})
            r.step, r.section = step, section[0]

            def level_in(which, slot):
                number = PLAN[which][base]
                for other in range(1, slots):
                    number = jnp.where(slot == other, PLAN[which][base + other], number)
                return number

            def level(slot):
                return jnp.where(r.section == 0, level_in(0, slot), level_in(1, slot))

            def copy(name, slot):
                kind, depth, micro = self.kinds[name]
                at = slot if depth > 1 else 0
                near = ref[name, 1].at[at]
                if kind == 0:
                    far = ref[name, 0].at[level(slot) if micro else base + slot]
                    pair = (far, near)
                else:
                    pair = (near, ref[name, 0].at[slot])
                return Item(lambda: pltpu.make_async_copy(*pair, ref[name, 2].at[at]), near)

            def start(*which):
                for n in which:
                    copy(n, step).start()

            def wait(*which):
                for n in which:
                    copy(n, step).wait()

            def at_first(act):
                if slots > 1:
                    pl.when(step == 0)(act)
                else:
                    act()

            def at_last(act):
                if slots > 1:
                    pl.when(step == slots - 1)(act)
                else:
                    act()

            r.level_of, r.level = level, level(step)
            r.copy, r.start, r.wait, r.at_first, r.at_last = copy, start, wait, at_first, at_last
            for n, (kind, depth, micro) in self.kinds.items():
                setattr(r, n, ref[n, 1].at[step if depth > 1 else 0])
                setattr(r, "all_" + n, (ref[n, 0], ref[n, 1]))
            body(r)

        results = pl.pallas_call(
            kernel,
            out_shape=self.outs,
            grid_spec=pltpu.PrefetchScalarGridSpec(
                num_scalar_prefetch=1,
                grid=(slots,),
                in_specs=self.in_specs,
                out_specs=self.out_specs,
                scratch_shapes=self.scratch,
            ),
            compiler_params=pltpu.CompilerParams(vmem_limit_bytes=self.limit),
            cost_estimate=pl.CostEstimate(
                flops=self.flops * slots, bytes_accessed=1 << 20, transcendentals=0
            ),
            name=name,
        )(self.section, *self.args)
        return SimpleNamespace(
            **{n[0] if isinstance(n, tuple) else n: v for n, v in zip(self.out_names, results)}
        )


class Fill:
    def __init__(self, own, got, target, sems, mine, pieces=1, dim=0):
        self.sources, self.target, self.sems, self.mine = (own, got), target, sems, mine
        self.pieces, self.dim = pieces, dim

    def _copy(self, source, piece):
        source = self.sources[source]
        if self.pieces == 1:
            return pltpu.make_async_copy(source, self.target, self.sems.at[0])
        size = self.target.shape[self.dim] // self.pieces
        cut = tuple(
            pl.ds(piece * size, size) if at == self.dim else slice(None)
            for at in range(len(self.target.shape))
        )
        return pltpu.make_async_copy(source.at[cut], self.target.at[cut], self.sems.at[piece])

    def start(self):
        for source, chosen_one in enumerate((self.mine, jnp.logical_not(self.mine))):

            @pl.when(chosen_one)
            def _():
                for piece in range(self.pieces):
                    self._copy(source, piece).start()

    def wait(self, piece=None):
        for at in range(self.pieces) if piece is None else (piece,):
            self._copy(0, at).wait()


def zero(*refs):
    for ref in refs:
        ref[...] = jnp.zeros_like(ref)


def valid_row(valid, level):
    row = valid[0:1, :]
    for other in range(1, valid.shape[0]):
        row = jnp.where(level == other, valid[other : other + 1, :], row)
    return row


def live_column(valid, level, live):
    row = jnp.where(valid_row(valid, level) > 0, 1.0, 0.0)
    row = jnp.broadcast_to(row, (8, row.shape[1])).astype(BF)
    live[...] = mm_tn(row, jnp.full((8, 128), 0.125, BF))[:, 0:1]


def adapter_of(mats, vecs, which):
    vec = vecs.at[which]
    return Adapter(
        mats.at[2 * which], vec[0:1, 0:64], mats.at[2 * which + 1], vec[1:2, :], vec[2:3, :], vec[3:4, :]
    )


def portions_shape(rows, width):
    return ((width // 128, rows, 2 * rows), BF)


def attn_saved(rows, width, hidden):
    return dict(
        packed=((rows, 3 * width), BF), context=((rows, width), BF), linv=((rows, width), BF)
    )


def norm_saved(rows, width):
    return dict(
        attended=((rows, width), BF),
        act1=((rows, 64), BF),
        slope1=((rows, 64), F32),
        std1=((rows, width), BF),
        scale1=((rows, 1), F32),
    )


def ffn_saved(rows, width, hidden):
    return dict(
        slope=((rows, hidden), BF),
        returned=((rows, width), BF),
        act2=((rows, 64), BF),
        slope2=((rows, 64), F32),
        std2=((rows, width), BF),
        scale2=((rows, 1), F32),
    )


STAT_ROWS = 8


def pair_copy(source, target, sems, pair, length):
    lanes = pl.ds(0, 2 * length)
    return pltpu.make_async_copy(
        source.at[pair, :, lanes], target.at[pair, :, lanes], sems.at[pair]
    )


def first_attn_forward(section, tokens, valid, own, got, sizes, slots):
    rows, width, hidden = sizes
    pairs = width // 128
    call = Call(section, slots)
    call.load(micro=True, h=tokens)
    call.whole(valid=valid)
    call.raw(own=own.qkv, got=got.qkv, own_out=own.out, got_out=got.out)
    call.whole(own_mats=own.mats, got_mats=got.mats, own_vecs=own.vecs, got_vecs=got.vecs)
    call.save(**attn_saved(*sizes), **norm_saved(rows, width), middle=((rows, width), BF))
    shape, dtype = portions_shape(rows, width)
    call.out(portions=((slots,) + shape, dtype))
    call.blocks(stats=((2, width), F32))
    call.temp(
        held=((slots,) + shape, dtype),
        live=((rows, 1), F32),
        bias=((rows, 256), F32),
        qkv=(own.qkv.shape, BF),
        out=(own.out.shape, BF),
        mats=(own.mats.shape, BF),
        vecs=(own.vecs.shape, F32),
    )
    call.sems(qkv_sems=3, out_sems=1, pair_sems=(slots, pairs))
    call.flops = 2 * rows * width * width * 12

    def body(r):
        mine = r.section == 0
        qkv = Fill(r.own, r.got, r.qkv, r.qkv_sems, mine, 3, 2)
        out = Fill(r.own_out, r.got_out, r.out, r.out_sems, mine)

        def begin():
            r.copy("h", 0).start()
            qkv.start()
            out.start()
            for slot in range(1, slots):
                r.copy("h", slot).start()
            zero(r.stats)
            r.mats[...] = jnp.where(mine, r.own_mats[...], r.got_mats[...])
            r.vecs[...] = jnp.where(mine, r.own_vecs[...], r.got_vecs[...])

        r.at_first(begin)
        live_column(r.valid, r.level, r.live)
        r.wait("h")
        qkv_phase(r.h, r.qkv.at[0], r.packed, lambda at: at % 3 or r.at_first(lambda: qkv.wait(at // 3)))
        r.start("packed")

        def pair_copy_of(slot, pair, length):
            return pair_copy(r.held.at[slot], r.portions.at[slot], r.pair_sems.at[slot], pair, length)

        attention_forward(
            r.level, r.valid, r.bias, r.packed, r.context, r.held.at[r.step], r.linv,
            lambda pair, length: pair_copy_of(r.step, pair, length).start(),
        )
        r.start("context", "linv")
        r.at_first(out.wait)
        project(r.context, r.out.at[0], r.attended)
        saved = (r.act1, r.slope1, r.std1, r.scale1)
        adapter_norm(
            r.h, r.attended, r.live, adapter_of(r.mats, r.vecs, 0), saved, r.middle, r.stats
        )
        r.start("middle", *norm_saved(rows, width))

        def finish():
            for slot in range(slots):
                for name in ("middle", *attn_saved(*sizes), *norm_saved(rows, width)):
                    r.copy(name, slot).wait()

                def waits(length):
                    for pair in range(pairs):
                        pair_copy_of(slot, pair, length).wait()

                by_level(r.level_of(slot), waits)

        r.at_last(finish)

    return call.run(body, "first_attn")


STAGE_ATTN0, STAGE_FFN0, STAGE_ATTN1, STAGE_FFN1 = range(4)


def middle_part(section, kept, cotangent, valid, own, got, sizes, slots):
    rows, width, hidden = sizes
    call = Call(section, slots)
    row = ((rows, width), BF)
    call.raw(base=kept.middle, cotangent=cotangent, **{"far_" + n: getattr(kept, n) for n in norm_saved(rows, width)})
    call.whole(valid=valid, stats=kept.stats)
    for name in ("qkv", "out", "win", "wout", "mats", "vecs"):
        call.raw(**{"own_" + name: getattr(own, name), "got_" + name: getattr(got, name)})
    call.temp(
        qkv=(own.qkv.shape, BF),
        win=(own.win.shape, BF),
        wout=(own.wout.shape, BF),
        outs=((2,) + own.out.shape, BF),
        mats=((2,) + own.mats.shape, BF),
        vecs=((2,) + own.vecs.shape, F32),
    )
    call.sems(win_sems=4, wout_sems=1, weight_sems=(8, 1), base_sems=1, up_sems=1, norm_sems=5)
    call.save(depth=1, result=row, dfirst0=row, dcontext0=row)
    grad_shape = (4, BLOCK_ROWS, width)
    call.temp(grads=((8,) + grad_shape[1:], F32))
    call.blocks(keep=(grad_shape, BF), send=(grad_shape, BF))
    call.temp(**attn_saved(*sizes))
    call.temp(
        attended=((4,) + row[0], BF),
        act1=((4, rows, 64), BF),
        slope1=((4, rows, 64), F32),
        std1=((4,) + row[0], BF),
        scale1=((4, rows, 1), F32),
        slope=((2, rows, hidden), BF),
        chain=((3,) + row[0], BF),
        sums=((4, 2, width), F32),
        up=row,
        held=portions_shape(rows, width),
        live=((rows, 1), F32),
        bias=((rows, 256), F32),
        wide=((rows, hidden), BF),
        dsum=((rows, width), F32),
        low=row,
        dpre=((rows, 64), BF),
        dinner=row,
    )
    call.flops = 12 * rows * width * (4 * width + 2 * hidden)
    norms = tuple(norm_saved(rows, width))

    def body(r):
        first, second = r.section == 0, r.section == 1

        def fill(name, target, at, mine):
            return Fill(
                getattr(r, "own_" + name), getattr(r, "got_" + name), target, r.weight_sems.at[at], mine
            )

        qkv, out1 = fill("qkv", r.qkv, 0, second), fill("out", r.outs.at[1], 1, second)
        mats1, vecs1 = fill("mats", r.mats.at[1], 2, second), fill("vecs", r.vecs.at[1], 3, second)
        out0 = fill("out", r.outs.at[0], 4, first)
        mats0, vecs0 = fill("mats", r.mats.at[0], 5, first), fill("vecs", r.vecs.at[0], 6, first)
        win0, win1 = (Fill(r.own_win, r.got_win, r.win, r.win_sems, m, 4, 2) for m in (first, second))
        wout0, wout1 = (Fill(r.own_wout, r.got_wout, r.wout, r.wout_sems, m) for m in (first, second))

        def base_copy(slot):
            return pltpu.make_async_copy(r.base.at[slot], r.chain.at[0], r.base_sems.at[0])

        def slot_copies():
            copies = [pltpu.make_async_copy(r.cotangent.at[r.level], r.up, r.up_sems.at[0])]
            for at, name in enumerate(norms):
                copies.append(
                    pltpu.make_async_copy(
                        getattr(r, "far_" + name).at[r.step], getattr(r, name).at[0], r.norm_sems.at[at]
                    )
                )
            return copies

        def begin():
            for item in (mats0, vecs0):
                item.start()
            base_copy(0).start()
            for item in (win0, wout0, qkv, out1, mats1, vecs1, out0):
                item.start()
            zero(r.grads, r.sums)
            for item in (mats0, vecs0, win0, wout0):
                item.wait()

        def later(act):
            pl.when(r.step > 0)(act)

        r.at_first(begin)
        for item in slot_copies():
            item.start()
        live_column(r.valid, r.level, r.live)
        base_copy(r.step).wait()
        later(lambda: r.copy("result", r.step - 1).wait())

        def saved_of(stage):
            return tuple(getattr(r, n).at[stage] for n in ("act1", "slope1", "std1", "scale1"))

        def adapter_at(stage):
            return adapter_of(r.mats.at[stage // 2], r.vecs.at[stage // 2], stage % 2)

        def forward(at, carry):
            stage = at + 1
            inner = r.attended.at[stage]
            here = r.chain.at[at]

            @pl.when(at == 1)
            def _():
                win1.start()
                wout1.start()
                for item in (qkv, out1, mats1, vecs1):
                    r.at_first(item.wait)
                qkv_phase(here, r.qkv.at[0], r.packed)
                attention_forward(r.level, r.valid, r.bias, r.packed, r.context, r.held, r.linv)
                project(r.context, r.outs.at[1, 0], inner)

            @pl.when(at != 1)
            def _():
                @pl.when(at == 2)
                def _():
                    win1.wait()
                    wout1.wait()

                ffn_forward(here, r.win.at[0], r.wout.at[0], r.wide, r.slope.at[stage // 2], inner)

            def norm(target):
                adapter_norm(
                    here, inner, r.live, adapter_at(stage), saved_of(stage), target, r.sums.at[stage]
                )

            norm(r.chain.at[lax.rem(at + 1, 3)])
            return carry

        lax.fori_loop(0, 3, forward, 0)
        r.result[...] = r.chain[0]
        r.start("result")

        @pl.when(r.step + 1 < slots)
        def _():
            base_copy(r.step + 1).start()

        for item in slot_copies():
            item.wait()

        def backward(at, carry):
            stage = 3 - at
            inner = r.attended.at[stage]

            @pl.when(stage % 2 == 1)
            def _():
                r.dsum[...] = r.up[...].astype(F32)

            norm_adapter_back(
                r.dsum, saved_of(stage), inner, adapter_at(stage), r.low, r.dpre, r.dinner,
                r.grads.at[2 * stage], r.grads.at[2 * stage + 1],
            )

            @pl.when(stage % 2 == 1)
            def _():
                @pl.when(at == 2)
                def _():
                    wout0.wait()
                    win0.wait()

                ffn_backward(r.dinner, r.win.at[0], r.wout.at[0], r.slope.at[stage // 2], r.wide, r.dsum)

            @pl.when(stage % 2 == 0)
            def _():
                @pl.when(at == 3)
                def _():
                    r.at_first(out0.wait)
                    later(lambda: r.copy("dfirst0", r.step - 1).wait())

                @pl.when(at == 1)
                def _():
                    wout0.start()
                    win0.start()
                    later(lambda: r.copy("dcontext0", r.step - 1).wait())

                project_back(r.dinner, r.outs.at[stage // 2, 0], r.dcontext0)

                @pl.when(at == 1)
                def _():
                    attention_backward(
                        r.level, r.packed, r.context, r.held, r.linv, r.dcontext0, r.packed
                    )
                    input_backward(r.packed, r.qkv.at[0], r.dsum, r.up)

            return carry

        lax.fori_loop(0, 4, backward, 0)
        r.dfirst0[...] = r.dsum[...].astype(BF)
        r.start("dfirst0", "dcontext0")

        def finish():
            r.wait("result", "dfirst0", "dcontext0")
            for layer in range(2):
                attn, ffn = r.sums.at[2 * layer], r.sums.at[2 * layer + 1]
                target = r.grads.at[4 * layer + ATTN_UP]
                if layer == 0:
                    attn = r.stats
                target[STATS : STATS + 1, :] = attn[0:1, :]
                target[STATS + 1 : STATS + 3, :] = ffn[...]
                count = jnp.zeros((1, 1), F32)
                for slot in range(slots):
                    row = jnp.where(valid_row(r.valid, r.level_of(slot)) > 0, 1.0, 0.0)
                    count += jnp.sum(row, axis=1, keepdims=True)
                target[STATS + 3 : STATS + 4, :] = jnp.broadcast_to(count, (1, width))
            for block in range(4):
                r.keep[block] = r.grads[4 * r.section + block].astype(BF)
                r.send[block] = r.grads[4 - 4 * r.section + block].astype(BF)

        r.at_last(finish)

    return call.run(body, "middle_part")


def first_attn_backward(section, back, there, kept, own, got, sizes, slots):
    rows, width, hidden = sizes
    pairs = width // 128
    call = Call(section, slots)
    call.load(packed=kept.packed, dcontext=back.dcontext0, context=kept.context, linv=kept.linv)
    call.load(dfirst=back.dfirst0)
    call.raw(portions=kept.portions, own=own.qkv, got=got.qkv, here=back.result, there=there)
    call.out(input_grad=((slots, rows, width), BF), result=((2 * slots, rows, width), BF))
    shape, dtype = portions_shape(rows, width)
    call.temp(
        held=((slots,) + shape, dtype),
        qkv=(own.qkv.shape, BF),
        stage=((2 * slots, rows, width), BF),
        dentry=((slots, rows, width), BF),
    )
    call.sems(
        qkv_sems=3, pair_sems=(slots, pairs), in_sems=2 * slots, out_sems=2 * slots, grad_sems=slots
    )
    call.flops = 2 * rows * width * width * 12

    def body(r):
        fill = Fill(r.own, r.got, r.qkv, r.qkv_sems, r.section == 0, 3, 1)

        def pair_copy_of(slot, pair, length):
            return pair_copy(r.portions.at[slot], r.held.at[slot], r.pair_sems.at[slot], pair, length)

        loads = ("packed", "dcontext", "context", "linv")
        ins, outs = [], []
        for at in range(slots):
            mine, other = (jnp.where(r.section == 0, PLAN[a][at], PLAN[1 - a][at]) for a in range(2))
            for source, target in ((r.here, mine), (r.there, other)):
                n = len(ins)
                ins.append(pltpu.make_async_copy(source.at[at], r.stage.at[n], r.in_sems.at[n]))
                outs.append(
                    pltpu.make_async_copy(r.stage.at[n], r.result.at[target], r.out_sems.at[n])
                )

        def begin():
            for slot in range(slots):
                for name in loads:
                    r.copy(name, slot).start()

                def starts(length):
                    for pair in range(pairs):
                        pair_copy_of(slot, pair, length).start()

                by_level(r.level_of(slot), starts)
                if slot == 0:
                    fill.start()
                r.copy("dfirst", slot).start()
            for item in ins:
                item.start()

        def grad_copy(slot):
            target = jnp.where(r.level_of(slot) % slots == 0, 0, 1)
            return pltpu.make_async_copy(
                r.dentry.at[slot], r.input_grad.at[target], r.grad_sems.at[slot]
            )

        r.at_first(begin)
        r.wait(*loads)
        attention_backward(
            r.level, r.packed, r.context, r.held.at[r.step], r.linv, r.dcontext, r.packed,
            r.step, pair_copy_of,
        )
        r.wait("dfirst")
        r.at_first(fill.wait)
        input_backward(r.packed, r.qkv.at[0], r.dfirst, r.dentry.at[r.step])
        grad_copy(r.step).start()

        def pass_on():
            for come, go in zip(ins, outs):
                come.wait()
                go.start()

        def finish():
            for slot in range(slots):
                grad_copy(slot).wait()
            for item in outs:
                item.wait()

        r.at_first(pass_on)
        r.at_last(finish)

    return call.run(body, "attn_back")


def packed_small(mats, vecs):
    width = mats[0].shape[-1]

    def kernel(*refs):
        sources, (out_mats, out_vecs) = refs[:-2], refs[-2:]
        for at in range(4):
            out_mats[at] = sources[at][0]
        out_vecs[...] = jnp.zeros_like(out_vecs)
        for at, ref in enumerate(sources[4:]):
            out_vecs[at // 4, at % 4 : at % 4 + 1, 0 : ref.shape[1]] = ref[...]

    return pl.pallas_call(
        kernel,
        out_shape=(
            jax.ShapeDtypeStruct((4, 64, width), BF),
            jax.ShapeDtypeStruct((2, 4, width), F32),
        ),
        name="pack",
    )(*mats, *vecs)


def unpacked(part, other, upper):
    width = part.shape[-1]
    matrix = jax.ShapeDtypeStruct((1, MATRIX_ROWS, width), F32)
    vector = jax.ShapeDtypeStruct((1, width), F32)
    small = jax.ShapeDtypeStruct((1, 64), F32)
    group = (matrix, small, matrix, vector, vector, vector)

    def kernel(upper, part, other, *outs):
        def block(at):
            mine = upper[0] == (1 if at >= 2 else 0)
            return jnp.where(mine, part[at % 2], other[at % 2]).astype(F32)

        for down, up, (mat_down, down_bias, mat_up, up_bias, gain, bias) in (
            (ATTN_DOWN, ATTN_UP, outs[:6]),
            (FFN_DOWN, FFN_UP, outs[6:12]),
        ):
            down, up = block(down), block(up)
            mat_down[0] = down[:MATRIX_ROWS]
            mat_up[0] = up[:MATRIX_ROWS]
            for row, target in ((UP_BIAS, up_bias), (GAIN, gain), (BIAS, bias), (DOWN_BIAS, down_bias)):
                target[...] = down[row : row + 1, : target.shape[1]]
        sums = block(ATTN_UP)[STATS : STATS + STAT_ROWS]
        means = jnp.sum(sums, axis=1, keepdims=True) / (sums[3:4, 0:1] * width)
        lane = lax.broadcasted_iota(jnp.int32, (1, 3), 1)
        picked = jnp.where(lane == 0, means[0:1], jnp.where(lane == 1, means[1:2], means[2:3]))
        outs[12][...] = jnp.sqrt(picked)

    vmem = pl.BlockSpec(memory_space=pltpu.VMEM)
    outs = pl.pallas_call(
        kernel,
        in_specs=[pl.BlockSpec(memory_space=pltpu.SMEM), vmem, vmem],
        out_shape=group * 2 + (jax.ShapeDtypeStruct((1, 3), F32),),
        name="unpack",
    )(upper.astype(jnp.int32).reshape(1), part, other)
    outs = list(outs)
    for at in (0, 6):
        outs[at] = jnp.swapaxes(outs[at], 1, 2)
    return tuple(outs)


def swap(value):
    return lax.ppermute(value, "section", [(0, 1), (1, 0)])


def after(value, *others):
    return lax.optimization_barrier((value,) + others)[0]


def exchanged(value, first_bit, second_bit):
    count = lax.axis_size("dp")
    pairs = [
        (section * count + at, section * count + (at ^ bit))
        for section, bit in enumerate((first_bit, second_bit))
        for at in range(count)
    ]
    return lax.ppermute(value, ("section", "dp"), pairs)


def summed_halves(part):
    section, mine = lax.axis_index("section"), lax.axis_index("dp")
    count = lax.axis_size("dp")
    halvings = ((1, 2), (2, 1))

    def is_upper(pair):
        return (mine & jnp.where(section == 0, pair[0], pair[1])) > 0

    for pair in halvings:
        upper = is_upper(pair)
        half = part.shape[0] // 2
        low, high = part[:half], part[half:]
        part = jnp.where(upper, high, low) + exchanged(jnp.where(upper, low, high), *pair)
    bit = 4
    while bit < count:
        part = part + exchanged(part, bit, bit)
        bit *= 2
    other, upper = exchanged(part, *halvings[1]), is_upper(halvings[1])
    part = jnp.concatenate([jnp.where(upper, other, part), jnp.where(upper, part, other)])
    return part, exchanged(part, *halvings[0]), is_upper(halvings[0])


def body(
    tokens, valid, cotangent, qkv, out, win, wout,
    attn_down, attn_down_bias, attn_up, attn_up_bias, gain1, bias1,
    ffn_down, ffn_down_bias, ffn_up, ffn_up_bias, gain2, bias2,
):
    section = lax.axis_index("section")
    micro_count, rows, width = tokens.shape
    sizes = (rows, width, win.shape[-1])
    slots = micro_count // 2
    mats, vecs = packed_small(
        (jnp.swapaxes(attn_down, 1, 2), attn_up, jnp.swapaxes(ffn_down, 1, 2), ffn_up),
        (attn_down_bias, attn_up_bias, gain1, bias1, ffn_down_bias, ffn_up_bias, gain2, bias2),
    )
    own = Layer(qkv, out, win, wout, mats, vecs)
    early = [swap(v) for v in (qkv, out, mats, vecs)]
    got_qkv, got_out, got_mats, got_vecs = early
    got_win, got_wout = (swap(after(v, *early)) for v in (win, wout))
    got = Layer(got_qkv, got_out, got_win, got_wout, got_mats, got_vecs)
    where = section.astype(jnp.int32).reshape(1)

    kept = first_attn_forward(where, tokens, valid, own, got, sizes, slots)
    back = middle_part(where, kept, cotangent, valid, own, got, sizes, slots)
    there = swap(back.result)

    part, other, upper = summed_halves(back.keep + swap(back.send))
    last = first_attn_backward(where, back, there, kept, own, got, sizes, slots)
    small = unpacked(part, after(other, last.input_grad), upper)
    return (last.result, last.input_grad) + small


def solution(mesh):
    rows = P(None, "dp", None)
    matrix, vector = P("section", None, None), P("section", None)
    weights = (matrix, vector, matrix, vector, vector, vector)
    return jax.shard_map(
        body,
        mesh=mesh,
        in_specs=(rows, P(None, "dp"), rows) + (matrix,) * 4 + weights * 2,
        out_specs=(rows, P("section", "dp", None)) + weights * 2 + (vector,),
        check_vma=False,
    )
```

profile of v0, /device:TPU:0, one launch (start us, length us, event | category | flops | bytes accessed | tf_op | source)
XLA Modules:
  0.0 214.1 jit_solution(3084379568900263739)
XLA Ops:
  0.7 0.5 collective-permute-start
  1.2 0.1 collective-permute-start.1
  1.2 1.9 pack.1
  3.1 0.4 collective-permute-start.2
  3.6 0.1 collective-permute-start.3
  3.7 5.9 %collective-permute-done.3.refs_9_.refs_20_ = f32[2,4,768]{2,1,0:T(4,128)S(1)} collective-permute-done((f32[2,4,768]{2,1,0:T(4,128)}, f32[2,4,768]{2,1,0:T(4,128)S(1)}, u32[]{:S(2)}, u32[]{:S(2)}) %collective-permute-start.3) | collective-permute-done | bytes 24608 | tf_op jit(solution)/shard_map/ppermute | solution.py:1052
  9.5 0.0 copy-start.5
  9.5 0.0 collective-permute-done.2.refs_7_.refs_18_
  9.5 0.0 copy-start.4
  9.5 0.0 collective-permute-done.1.refs_5_.refs_12_
  9.6 0.0 collective-permute-done.refs_3_.refs_10_.refs_7_
  9.6 0.7 copy-done.4
  10.3 0.0 copy-start.2
  10.3 0.4 collective-permute-start.4
  10.7 0.0 copy-done.5
  10.7 0.1 collective-permute-start.5
  10.8 1.4 copy-done.2
  12.2 22.0 %first_attn.1 = (bf16[2,512,2304]{2,1,0:T(8,128)(2,1)}, bf16[2,512,768]{2,1,0:T(8,128)(2,1)}, bf16[2,512,768]{2,1,0:T(8,128)(2,1)}, bf16[2,512,768]{2,1,0:T(8,12...) custom-call(s32[1]{0:T(128)} %bitcast.section, ...), custom_call_target="tpu_custom_call" | custom-call | flops 14495514624 | bytes 1048576 | tf_op jit(solution)/shard_map/first_attn/pallas_call | solution.py:493
  34.2 0.0 collective-permute-done.4.refs_14_
  34.2 0.0 collective-permute-done.5.refs_16_
  34.2 112.8 %middle_part.1 = (bf16[2,512,768]{2,1,0:T(8,128)(2,1)}, bf16[2,512,768]{2,1,0:T(8,128)(2,1)}, bf16[2,512,768]{2,1,0:T(8,128)(2,1)}, bf16[4,72,768]{2,1,0:T(8,128)(2,1)}, bf16[4,72,768]{2,1,0:T(8,128)(2,1)}) custom-call(s32[1]{0:T(128)} %bitcast.section, bf16[2,512,768]{2,1,0:T(8,128)(2,1)} %get-tuple-element.54.refs_0_, bf16[4,512,768]{2,1,0:T(8,128)(2,1)} %refs_1_.5, ...), custom_call_target="tpu_custom_call" | custom-call | flops 86973087744 | bytes 1048576 | tf_op jit(solution)/shard_map/middle_part/pallas_call | solution.py:493
  147.0 0.0 copy-start.3
  147.0 5.2 %collective-permute-start.7 = (bf16[4,72,768]{2,1,0:T(8,128)(2,1)}, bf16[4,72,768]{2,1,0:T(8,128)(2,1)S(1)}, u32[]{:S(2)}, u32[]{:S(2)}) collective-permute-start(bf16[4,72,768]{2,1,0:T(8,128)(2,1)} %get-tuple-element.72), channel_id=1, source_target_pairs={{0,16},{16,0},{1,17},{17,1},{2,18},{18,2},{3,19},{19,3},{4,20},{20... | collective-permute-start | bytes 1327112 | tf_op jit(solution)/shard_map/ppermute | solution.py:1052
  152.2 1.6 collective-permute-done.7
  153.8 1.1 add.15
  155.0 2.7 %collective-permute-start.8 = (bf16[2,72,768]{2,1,0:T(8,128)(2,1)S(1)}, bf16[2,72,768]{2,1,0:T(8,128)(2,1)S(1)}, u32[]{:S(2)}, u32[]{:S(2)}) collective-permute-start(bf16[2,72,768]{2,1,0:T(8,128)(2,1)S(1)} %broadcast_select_fusion), channel_id=1, source_target_pairs={{0,1},{1,0},{2,3},{3,2},{4,5},{5,4},{6,7},{7,6},{8,9},{9,8},{10,11... | collective-permute-start | bytes 663560 | tf_op jit(solution)/shard_map/ppermute | solution.py:1066
  157.7 0.0 copy-done.3
  157.7 0.1 collective-permute-start.6
  157.8 3.8 %collective-permute-done.8 = bf16[2,72,768]{2,1,0:T(8,128)(2,1)S(1)} collective-permute-done((bf16[2,72,768]{2,1,0:T(8,128)(2,1)S(1)}, bf16[2,72,768]{2,1,0:T(8,128)(2,1)S(1)}, u32[]{:S(2)}, u32[]{:S(2)}) %collective-permute-start.8) | collective-permute-done | bytes 221216 | tf_op jit(solution)/shard_map/ppermute | solution.py:1066
  161.6 2.1 collective-permute-start.9
  163.8 2.7 %collective-permute-done.9 = bf16[1,72,768]{2,1,0:T(8,128)(2,1)S(1)} collective-permute-done((bf16[1,72,768]{2,1,0:T(8,128)(2,1)S(1)}, bf16[1,72,768]{2,1,0:T(8,128)(2,1)S(1)}, u32[]{:S(2)}, u32[]{:S(2)}) %collective-permute-start.9) | collective-permute-done | bytes 110624 | tf_op jit(solution)/shard_map/ppermute | solution.py:1066
  166.5 2.1 collective-permute-start.10
  168.6 2.7 %collective-permute-done.10 = bf16[1,72,768]{2,1,0:T(8,128)(2,1)S(1)} collective-permute-done((bf16[1,72,768]{2,1,0:T(8,128)(2,1)S(1)}, bf16[1,72,768]{2,1,0:T(8,128)(2,1)S(1)}, u32[]{:S(2)}, u32[]{:S(2)}) %collective-permute-start.10) | collective-permute-done | bytes 110624 | tf_op jit(solution)/shard_map/ppermute | solution.py:1066
  171.4 3.3 %collective-permute-start.11 = (bf16[1,72,768]{2,1,0:T(8,128)(2,1)S(1)}, bf16[1,72,768]{2,1,0:T(8,128)(2,1)S(1)}, u32[]{:S(2)}, u32[]{:S(2)}) collective-permute-start(bf16[1,72,768]{2,1,0:T(8,128)(2,1)S(1)} %add.18), channel_id=1, source_target_pairs={{0,8},{1,9},{2,10},{3,11},{4,12},{5,13},{6,14},{7,15},{8,0},{9,1},... | collective-permute-start | bytes 331784 | tf_op jit(solution)/shard_map/ppermute | solution.py:1066
  174.7 2.7 %collective-permute-done.11 = bf16[1,72,768]{2,1,0:T(8,128)(2,1)S(1)} collective-permute-done((bf16[1,72,768]{2,1,0:T(8,128)(2,1)S(1)}, bf16[1,72,768]{2,1,0:T(8,128)(2,1)S(1)}, u32[]{:S(2)}, u32[]{:S(2)}) %collective-permute-start.11) | collective-permute-done | bytes 110624 | tf_op jit(solution)/shard_map/ppermute | solution.py:1066
  177.5 2.9 %collective-permute-start.12 = (bf16[1,72,768]{2,1,0:T(8,128)(2,1)S(1)}, bf16[1,72,768]{2,1,0:T(8,128)(2,1)S(1)}, u32[]{:S(2)}, u32[]{:S(2)}) collective-permute-start(bf16[1,72,768]{2,1,0:T(8,128)(2,1)S(1)} %add.19), channel_id=1, source_target_pairs={{0,2},{1,3},{2,0},{3,1},{4,6},{5,7},{6,4},{7,5},{8,10},{9,11},{10,... | collective-permute-start | bytes 331784 | tf_op jit(solution)/shard_map/ppermute | solution.py:1066
  180.4 3.8 %collective-permute-done.12 = bf16[1,72,768]{2,1,0:T(8,128)(2,1)S(1)} collective-permute-done((bf16[1,72,768]{2,1,0:T(8,128)(2,1)S(1)}, bf16[1,72,768]{2,1,0:T(8,128)(2,1)S(1)}, u32[]{:S(2)}, u32[]{:S(2)}) %collective-permute-start.12) | collective-permute-done | bytes 110624 | tf_op jit(solution)/shard_map/ppermute | solution.py:1066
  184.3 0.0 copy-start
  184.3 1.4 collective-permute-start.13
  185.7 0.0 collective-permute-done.6.refs_9_
  185.7 25.5 %attn_back.1 = (bf16[2,512,768]{2,1,0:T(8,128)(2,1)}, bf16[4,512,768]{2,1,0:T(8,128)(2,1)}) custom-call(s32[1]{0:T(128)} %bitcast.section, bf16[2,512,2304]{2,1,0:T(8,128)(2,1)} %get-tuple-element.53.refs_0_, bf16[2,512,768]{2,1,0:T(8,128)(2,1)} %get-tuple-element.63.refs_1_, bf16[2,512,768]{2,1,0:T(8,128)(2,1)} %get-tuple-element.64.refs_2_, ...), custom_call_target="tpu_custom_call" | custom-call | flops 14495514624 | bytes 1048576 | tf_op jit(solution)/shard_map/attn_back/pallas_call | solution.py:493
  211.3 0.0 copy-done
  211.3 0.0 collective-permute-done.13.other
  211.3 0.0 copy-start.1
  211.3 0.7 copy-done.1
  212.0 2.0 unpack.1
  (8 shorter events, 0.2 us)
Async XLA Ops:
  0.7 8.9 %collective-permute-start = (bf16[1,768,2304]{2,1,0:T(8,128)(2,1)}, bf16[1,768,2304]{2,1,0:T(8,128)(2,1)S(1)}, u32[]{:S(2)}, u32[]{:S(2)}) collective-permute-start(bf16[1,768,2304]{2,1,0:T(8,128)(2,1)} %refs_6_.3), channel_id=1, source_target_pairs={{0,16},{16,0},{1,17},{17,1},{2,18},{18,2},{3,19},{19,3},{4,20},{20... | collective-permute-start | bytes 10616840 | tf_op jit(solution)/shard_map/ppermute | solution.py:1052
  1.2 8.4 %collective-permute-start.1 = (bf16[1,768,768]{2,1,0:T(8,128)(2,1)}, bf16[1,768,768]{2,1,0:T(8,128)(2,1)}, u32[]{:S(2)}, u32[]{:S(2)}) collective-permute-start(bf16[1,768,768]{2,1,0:T(8,128)(2,1)} %refs_11_.3), channel_id=1, source_target_pairs={{0,16},{16,0},{1,17},{17,1},{2,18},{18,2},{3,19},{19,3},{4,20},{20... | collective-permute-start | bytes 3538952 | tf_op jit(solution)/shard_map/ppermute | solution.py:1052
  3.1 6.4 %collective-permute-start.2 = (bf16[4,64,768]{2,1,0:T(8,128)(2,1)}, bf16[4,64,768]{2,1,0:T(8,128)(2,1)S(1)}, u32[]{:S(2)}, u32[]{:S(2)}) collective-permute-start(bf16[4,64,768]{2,1,0:T(8,128)(2,1)} %get-tuple-element.51.refs_6_.refs_17_), channel_id=1, source_target_pairs={{0,16},{16,0},{1,17},{17,1},{2,18},{18,2},{3,19},{19,3},{4,20},{20... | collective-permute-start | bytes 1179656 | tf_op jit(solution)/shard_map/ppermute | solution.py:1052
  3.6 5.9 %collective-permute-start.3 = (f32[2,4,768]{2,1,0:T(4,128)}, f32[2,4,768]{2,1,0:T(4,128)S(1)}, u32[]{:S(2)}, u32[]{:S(2)}) collective-permute-start(f32[2,4,768]{2,1,0:T(4,128)} %get-tuple-element.52.refs_8_.refs_19_), channel_id=1, source_target_pairs={{0,16},{16,0},{1,17},{17,1},{2,18},{18,2},{3,19},{19,3},{4,20},{20... | collective-permute-start | bytes 73736 | tf_op jit(solution)/shard_map/ppermute | solution.py:1052
  9.5 1.2 copy-start.5
  9.5 0.8 copy-start.4
  10.3 1.9 copy-start.2
  10.3 23.9 %collective-permute-start.4 = (bf16[1,768,3072]{2,1,0:T(8,128)(2,1)}, bf16[1,768,3072]{2,1,0:T(8,128)(2,1)}, u32[]{:S(2)}, u32[]{:S(2)}) collective-permute-start(bf16[1,768,3072]{2,1,0:T(8,128)(2,1)} %refs_13_.1), channel_id=1, source_target_pairs={{0,16},{16,0},{1,17},{17,1},{2,18},{18,2},{3,19},{19,3},{4,20},{20... | collective-permute-start | bytes 14155784 | tf_op jit(solution)/shard_map/ppermute | solution.py:1052
  10.7 23.5 %collective-permute-start.5 = (bf16[1,3072,768]{2,1,0:T(8,128)(2,1)}, bf16[1,3072,768]{2,1,0:T(8,128)(2,1)}, u32[]{:S(2)}, u32[]{:S(2)}) collective-permute-start(bf16[1,3072,768]{2,1,0:T(8,128)(2,1)} %refs_15_.1), channel_id=1, source_target_pairs={{0,16},{16,0},{1,17},{17,1},{2,18},{18,2},{3,19},{19,3},{4,20},{20... | collective-permute-start | bytes 14155784 | tf_op jit(solution)/shard_map/ppermute | solution.py:1052
  147.0 10.7 %copy-start.3 = (bf16[2,512,768]{2,1,0:T(8,128)(2,1)S(1)}, bf16[2,512,768]{2,1,0:T(8,128)(2,1)}, u32[]{:S(2)}) copy-start(bf16[2,512,768]{2,1,0:T(8,128)(2,1)} %get-tuple-element.68.refs_8_) | copy-start | bytes 4718596
  147.0 6.8 %collective-permute-start.7 = (bf16[4,72,768]{2,1,0:T(8,128)(2,1)}, bf16[4,72,768]{2,1,0:T(8,128)(2,1)S(1)}, u32[]{:S(2)}, u32[]{:S(2)}) collective-permute-start(bf16[4,72,768]{2,1,0:T(8,128)(2,1)} %get-tuple-element.72), channel_id=1, source_target_pairs={{0,16},{16,0},{1,17},{17,1},{2,18},{18,2},{3,19},{19,3},{4,20},{20... | collective-permute-start | bytes 1327112 | tf_op jit(solution)/shard_map/ppermute | solution.py:1052
  155.0 6.6 %collective-permute-start.8 = (bf16[2,72,768]{2,1,0:T(8,128)(2,1)S(1)}, bf16[2,72,768]{2,1,0:T(8,128)(2,1)S(1)}, u32[]{:S(2)}, u32[]{:S(2)}) collective-permute-start(bf16[2,72,768]{2,1,0:T(8,128)(2,1)S(1)} %broadcast_select_fusion), channel_id=1, source_target_pairs={{0,1},{1,0},{2,3},{3,2},{4,5},{5,4},{6,7},{7,6},{8,9},{9,8},{10,11... | collective-permute-start | bytes 663560 | tf_op jit(solution)/shard_map/ppermute | solution.py:1066
  157.7 28.0 %collective-permute-start.6 = (bf16[2,512,768]{2,1,0:T(8,128)(2,1)S(1)}, bf16[2,512,768]{2,1,0:T(8,128)(2,1)}, u32[]{:S(2)}, u32[]{:S(2)}) collective-permute-start(bf16[2,512,768]{2,1,0:T(8,128)(2,1)S(1)} %copy-done.3), channel_id=1, source_target_pairs={{0,16},{16,0},{1,17},{17,1},{2,18},{18,2},{3,19},{19,3},{4,20},{20... | collective-permute-start | bytes 4718600 | tf_op jit(solution)/shard_map/ppermute | solution.py:1052
  161.6 4.8 %collective-permute-start.9 = (bf16[1,72,768]{2,1,0:T(8,128)(2,1)S(1)}, bf16[1,72,768]{2,1,0:T(8,128)(2,1)S(1)}, u32[]{:S(2)}, u32[]{:S(2)}) collective-permute-start(bf16[1,72,768]{2,1,0:T(8,128)(2,1)S(1)} %broadcast_select_fusion.3), channel_id=1, source_target_pairs={{0,2},{1,3},{2,0},{3,1},{4,6},{5,7},{6,4},{7,5},{8,10},{9,11},{10,... | collective-permute-start | bytes 331784 | tf_op jit(solution)/shard_map/ppermute | solution.py:1066
  166.5 4.9 %collective-permute-start.10 = (bf16[1,72,768]{2,1,0:T(8,128)(2,1)S(1)}, bf16[1,72,768]{2,1,0:T(8,128)(2,1)S(1)}, u32[]{:S(2)}, u32[]{:S(2)}) collective-permute-start(bf16[1,72,768]{2,1,0:T(8,128)(2,1)S(1)} %select_add_fusion.1), channel_id=1, source_target_pairs={{0,4},{1,5},{2,6},{3,7},{4,0},{5,1},{6,2},{7,3},{8,12},{9,13},{10,... | collective-permute-start | bytes 331784 | tf_op jit(solution)/shard_map/ppermute | solution.py:1066
  171.4 6.0 %collective-permute-start.11 = (bf16[1,72,768]{2,1,0:T(8,128)(2,1)S(1)}, bf16[1,72,768]{2,1,0:T(8,128)(2,1)S(1)}, u32[]{:S(2)}, u32[]{:S(2)}) collective-permute-start(bf16[1,72,768]{2,1,0:T(8,128)(2,1)S(1)} %add.18), channel_id=1, source_target_pairs={{0,8},{1,9},{2,10},{3,11},{4,12},{5,13},{6,14},{7,15},{8,0},{9,1},... | collective-permute-start | bytes 331784 | tf_op jit(solution)/shard_map/ppermute | solution.py:1066
  177.5 6.7 %collective-permute-start.12 = (bf16[1,72,768]{2,1,0:T(8,128)(2,1)S(1)}, bf16[1,72,768]{2,1,0:T(8,128)(2,1)S(1)}, u32[]{:S(2)}, u32[]{:S(2)}) collective-permute-start(bf16[1,72,768]{2,1,0:T(8,128)(2,1)S(1)} %add.19), channel_id=1, source_target_pairs={{0,2},{1,3},{2,0},{3,1},{4,6},{5,7},{6,4},{7,5},{8,10},{9,11},{10,... | collective-permute-start | bytes 331784 | tf_op jit(solution)/shard_map/ppermute | solution.py:1066
  184.3 27.0 %copy-start = (bf16[2,72,768]{2,1,0:T(8,128)(2,1)}, bf16[2,72,768]{2,1,0:T(8,128)(2,1)S(1)}, u32[]{:S(2)}) copy-start(bf16[2,72,768]{2,1,0:T(8,128)(2,1)S(1)} %pad_maximum_fusion.part) | copy-start | bytes 663556
  184.3 27.0 %collective-permute-start.13 = (bf16[2,72,768]{2,1,0:T(8,128)(2,1)S(1)}, bf16[2,72,768]{2,1,0:T(8,128)(2,1)S(1)}, u32[]{:S(2)}, u32[]{:S(2)}) collective-permute-start(bf16[2,72,768]{2,1,0:T(8,128)(2,1)S(1)} %pad_maximum_fusion.part), channel_id=1, source_target_pairs={{0,1},{1,0},{2,3},{3,2},{4,5},{5,4},{6,7},{7,6},{8,9},{9,8},{10,11... | collective-permute-start | bytes 663560 | tf_op jit(solution)/shard_map/ppermute | solution.py:1066
  211.3 0.7 copy-start.1
where the time goes:
time: 214 us
  Pallas kernels  164 us (77%)
  waiting for transfers between devices  23.4 us (11%)
  starting transfers between devices  21.5 us (10%)
  local copies, waits for them, and re-layouts  2.8 us (1%)
    pallas_call x3, Pallas kernels, run(): pl.pallas_call(kernel, out_shape=self.outs, grid_spec=pltpu.PrefetchScala...  160 us
    ppermute x6, waiting for transfers between devices, exchanged(): return lax.ppermute(value, ('section', 'dp'), pairs)  15.8 us
    ppermute x6, starting transfers between devices, exchanged(): return lax.ppermute(value, ('section', 'dp'), pairs)  14.6 us
    ppermute x8, waiting for transfers between devices, swap(): return lax.ppermute(value, 'section', [(0, 1), (1, 0)])  7.54 us
    ppermute x8, starting transfers between devices, swap(): return lax.ppermute(value, 'section', [(0, 1), (1, 0)])  6.95 us
  transfers between devices with their start and end apart: 14, of which 7 were waited for; matrix products, arithmetic and copies ran while one was open for 0% of the time, Pallas kernels for 23%

commit v1 on v0

--- a/solution.py
+++ b/solution.py
@@ -21,6 +21,7 @@
 F32 = jnp.float32
 ANY = pl.BlockSpec(memory_space=pl.ANY)
 VMEM_LIMIT = 60 << 20
+SMALL_LIMIT = 16 << 20
 
 ATTN_DOWN, ATTN_UP, FFN_DOWN, FFN_UP = range(4)
 MATRIX_ROWS, BLOCK_ROWS = 64, 72
@@ -77,7 +78,7 @@
     lax.fori_loop(0, count // unroll, some, 0)
 
 
-PAIRS_FORWARD, PAIRS_BACKWARD = 2, 1
+PAIRS_FORWARD, PAIRS_BACKWARD = 3, 1
 FFN_FORWARD, FFN_BACKWARD = 12, 12
 
 
@@ -613,7 +614,7 @@
     call.load(micro=True, h=tokens)
     call.whole(valid=valid)
     call.raw(own=own.qkv, got=got.qkv, own_out=own.out, got_out=got.out)
-    call.whole(own_mats=own.mats, got_mats=got.mats, own_vecs=own.vecs, got_vecs=got.vecs)
+    call.raw(own_mats=own.mats, got_mats=got.mats, own_vecs=own.vecs, got_vecs=got.vecs)
     call.save(**attn_saved(*sizes), **norm_saved(rows, width), middle=((rows, width), BF))
     shape, dtype = portions_shape(rows, width)
     call.out(portions=((slots,) + shape, dtype))
@@ -627,23 +628,23 @@
         mats=(own.mats.shape, BF),
         vecs=(own.vecs.shape, F32),
     )
-    call.sems(qkv_sems=3, out_sems=1, pair_sems=(slots, pairs))
+    call.sems(qkv_sems=3, out_sems=1, mats_sems=1, vecs_sems=1, pair_sems=(slots, pairs))
     call.flops = 2 * rows * width * width * 12
 
     def body(r):
         mine = r.section == 0
         qkv = Fill(r.own, r.got, r.qkv, r.qkv_sems, mine, 3, 2)
         out = Fill(r.own_out, r.got_out, r.out, r.out_sems, mine)
+        mats = Fill(r.own_mats, r.got_mats, r.mats, r.mats_sems, mine)
+        vecs = Fill(r.own_vecs, r.got_vecs, r.vecs, r.vecs_sems, mine)
 
         def begin():
             r.copy("h", 0).start()
-            qkv.start()
-            out.start()
+            for item in (qkv, out, mats, vecs):
+                item.start()
             for slot in range(1, slots):
                 r.copy("h", slot).start()
             zero(r.stats)
-            r.mats[...] = jnp.where(mine, r.own_mats[...], r.got_mats[...])
-            r.vecs[...] = jnp.where(mine, r.own_vecs[...], r.got_vecs[...])
 
         r.at_first(begin)
         live_column(r.valid, r.level, r.live)
@@ -659,7 +660,7 @@
             lambda pair, length: pair_copy_of(r.step, pair, length).start(),
         )
         r.start("context", "linv")
-        r.at_first(out.wait)
+        r.at_first(lambda: [item.wait() for item in (out, mats, vecs)] and None)
         project(r.context, r.out.at[0], r.attended)
         saved = (r.act1, r.slope1, r.std1, r.scale1)
         adapter_norm(
@@ -1008,17 +1009,21 @@
     )(*mats, *vecs)
 
 
-def unpacked(part, other, upper):
-    width = part.shape[-1]
+def unpacked(quarters, member):
+    width = quarters[0].shape[-1]
     matrix = jax.ShapeDtypeStruct((1, MATRIX_ROWS, width), F32)
     vector = jax.ShapeDtypeStruct((1, width), F32)
     small = jax.ShapeDtypeStruct((1, 64), F32)
     group = (matrix, small, matrix, vector, vector, vector)
 
-    def kernel(upper, part, other, *outs):
+    def kernel(member, *refs):
+        sources, outs = refs[:4], refs[4:]
+
         def block(at):
-            mine = upper[0] == (1 if at >= 2 else 0)
-            return jnp.where(mine, part[at % 2], other[at % 2]).astype(F32)
+            picked = sources[0][...]
+            for d in (1, 2, 3):
+                picked = jnp.where((member[0] ^ at) == d, sources[d][...], picked)
+            return picked.astype(F32)
 
         for down, up, (mat_down, down_bias, mat_up, up_bias, gain, bias) in (
             (ATTN_DOWN, ATTN_UP, outs[:6]),
@@ -1038,10 +1043,11 @@
     vmem = pl.BlockSpec(memory_space=pltpu.VMEM)
     outs = pl.pallas_call(
         kernel,
-        in_specs=[pl.BlockSpec(memory_space=pltpu.SMEM), vmem, vmem],
+        in_specs=[pl.BlockSpec(memory_space=pltpu.SMEM)] + [vmem] * 4,
         out_shape=group * 2 + (jax.ShapeDtypeStruct((1, 3), F32),),
+        compiler_params=pltpu.CompilerParams(vmem_limit_bytes=SMALL_LIMIT),
         name="unpack",
-    )(upper.astype(jnp.int32).reshape(1), part, other)
+    )(member.astype(jnp.int32).reshape(1), *quarters)
     outs = list(outs)
     for at in (0, 6):
         outs[at] = jnp.swapaxes(outs[at], 1, 2)
@@ -1056,36 +1062,28 @@
     return lax.optimization_barrier((value,) + others)[0]
 
 
-def exchanged(value, first_bit, second_bit):
+def exchanged(value, bits):
     count = lax.axis_size("dp")
-    pairs = [
-        (section * count + at, section * count + (at ^ bit))
-        for section, bit in enumerate((first_bit, second_bit))
-        for at in range(count)
-    ]
-    return lax.ppermute(value, ("section", "dp"), pairs)
-
-
-def summed_halves(part):
-    section, mine = lax.axis_index("section"), lax.axis_index("dp")
-    count = lax.axis_size("dp")
-    halvings = ((1, 2), (2, 1))
-
-    def is_upper(pair):
-        return (mine & jnp.where(section == 0, pair[0], pair[1])) > 0
-
-    for pair in halvings:
-        upper = is_upper(pair)
-        half = part.shape[0] // 2
-        low, high = part[:half], part[half:]
-        part = jnp.where(upper, high, low) + exchanged(jnp.where(upper, low, high), *pair)
+    return lax.ppermute(value, "dp", [(at, at ^ bits) for at in range(count)])
+
+
+def summed_quarters(part):
+    mine, count = lax.axis_index("dp"), lax.axis_size("dp")
+    member = mine & 3
+
+    def quarter(d):
+        return lax.dynamic_index_in_dim(part, member ^ d, 0, keepdims=False)
+
+    def together(own, a, b, c):
+        own, a, b, c = (v.astype(F32) for v in (own, a, b, c))
+        return ((own + a) + (b + c)).astype(BF)
+
+    total = together(quarter(0), *(exchanged(quarter(d), d) for d in (1, 2, 3)))
     bit = 4
     while bit < count:
-        part = part + exchanged(part, bit, bit)
+        total = total + exchanged(total, bit)
         bit *= 2
-    other, upper = exchanged(part, *halvings[1]), is_upper(halvings[1])
-    part = jnp.concatenate([jnp.where(upper, other, part), jnp.where(upper, part, other)])
-    return part, exchanged(part, *halvings[0]), is_upper(halvings[0])
+    return [total] + [exchanged(total, d) for d in (1, 2, 3)], member
 
 
 def body(
@@ -1112,9 +1110,9 @@
     back = middle_part(where, kept, cotangent, valid, own, got, sizes, slots)
     there = swap(back.result)
 
-    part, other, upper = summed_halves(back.keep + swap(back.send))
+    quarters, member = summed_quarters(back.keep + swap(back.send))
     last = first_attn_backward(where, back, there, kept, own, got, sizes, slots)
-    small = unpacked(part, after(other, last.input_grad), upper)
+    small = unpacked([quarters[0]] + [after(v, last.input_grad) for v in quarters[1:]], member)
     return (last.result, last.input_grad) + small
 
 

time: 214 us -> 209 us (0.977)
  Pallas kernels: 164 us -> 161 us
  starting transfers between devices: 21.5 us -> 19.3 us
    ppermute x6 -> x8, waiting for transfers between devices: 15.8 us -> 13 us  [exchanged(): return lax.ppermute(value, 'dp', [(at, at ^ bits) for at in range(count)])]
    ppermute x8, waiting for transfers between devices: 7.54 us -> 9.72 us  [swap(): return lax.ppermute(value, 'section', [(0, 1), (1, 0)])]
    ppermute x6 -> x8, starting transfers between devices: 14.6 us -> 12.5 us  [exchanged(): return lax.ppermute(value, 'dp', [(at, at ^ bits) for at in range(count)])]
  transfers between devices with their start and end apart: 14 -> 16, of which waited for: 7 -> 6; matrix products, arithmetic and copies ran while one was open for 0% -> 1% of each run, Pallas kernels for 23% -> 23%
where the time goes in v1:
time: 209 us
  Pallas kernels  161 us (77%)
  waiting for transfers between devices  22.7 us (11%)
  starting transfers between devices  19.3 us (9%)
  local copies, waits for them, and re-layouts  3.33 us (2%)
    pallas_call x3, Pallas kernels, run(): pl.pallas_call(kernel, out_shape=self.outs, grid_spec=pltpu.PrefetchScala...  158 us
    ppermute x8, waiting for transfers between devices, exchanged(): return lax.ppermute(value, 'dp', [(at, at ^ bits) for at in range(count)])  13 us
    ppermute x8, starting transfers between devices, exchanged(): return lax.ppermute(value, 'dp', [(at, at ^ bits) for at in range(count)])  12.5 us
    ppermute x8, waiting for transfers between devices, swap(): return lax.ppermute(value, 'section', [(0, 1), (1, 0)])  9.72 us
    ppermute x8, starting transfers between devices, swap(): return lax.ppermute(value, 'section', [(0, 1), (1, 0)])  6.85 us
  transfers between devices with their start and end apart: 16, of which 6 were waited for; matrix products, arithmetic and copies ran while one was open for 1% of the time, Pallas kernels for 23%

profile of v1, /device:TPU:0, one launch (start us, length us, event | category | flops | bytes accessed | tf_op | source)
XLA Modules:
  0.0 208.6 jit_solution(9783944849147691203)
XLA Ops:
  0.6 0.5 collective-permute-start
  1.2 0.1 collective-permute-start.1
  1.2 1.9 pack.1
  3.1 0.4 collective-permute-start.2
  3.6 0.1 collective-permute-start.3
  3.7 5.9 %collective-permute-done.3.refs_9_.refs_20_ = f32[2,4,768]{2,1,0:T(4,128)S(1)} collective-permute-done((f32[2,4,768]{2,1,0:T(4,128)}, f32[2,4,768]{2,1,0:T(4,128)S(1)}, u32[]{:S(2)}, u32[]{:S(2)}) %collective-permute-start.3) | collective-permute-done | bytes 24608 | tf_op jit(solution)/shard_map/ppermute | solution.py:1058
  9.5 0.0 copy-start.3
  9.5 0.0 collective-permute-done.2.refs_7_.refs_18_
  9.5 0.0 copy-start.2
  9.5 0.0 collective-permute-done.1.refs_5_.refs_12_
  9.6 0.0 collective-permute-done.refs_3_.refs_10_.refs_7_
  9.6 0.7 copy-done.2
  10.3 0.0 copy-start
  10.3 0.4 collective-permute-start.4
  10.7 0.0 copy-done.3
  10.7 0.1 collective-permute-start.5
  10.8 1.4 copy-done
  12.2 20.6 %first_attn.1 = (bf16[2,512,2304]{2,1,0:T(8,128)(2,1)}, bf16[2,512,768]{2,1,0:T(8,128)(2,1)}, bf16[2,512,768]{2,1,0:T(8,128)(2,1)}, bf16[2,512,768]{2,1,0:T(8,12...) custom-call(s32[1]{0:T(128)} %bitcast.section, ...), custom_call_target="tpu_custom_call" | custom-call | flops 14495514624 | bytes 1048576 | tf_op jit(solution)/shard_map/first_attn/pallas_call | solution.py:494
  32.8 0.0 collective-permute-done.4.refs_14_
  32.8 0.0 collective-permute-done.5.refs_16_
  32.8 112.1 %middle_part.1 = (bf16[2,512,768]{2,1,0:T(8,128)(2,1)}, bf16[2,512,768]{2,1,0:T(8,128)(2,1)}, bf16[2,512,768]{2,1,0:T(8,128)(2,1)}, bf16[4,72,768]{2,1,0:T(8,128)(2,1)}, bf16[4,72,768]{2,1,0:T(8,128)(2,1)}) custom-call(s32[1]{0:T(128)} %bitcast.section, bf16[2,512,768]{2,1,0:T(8,128)(2,1)} %get-tuple-element.56.refs_0_, bf16[4,512,768]{2,1,0:T(8,128)(2,1)} %refs_1_.5, ...), custom_call_target="tpu_custom_call" | custom-call | flops 86973087744 | bytes 1048576 | tf_op jit(solution)/shard_map/middle_part/pallas_call | solution.py:494
  145.0 5.2 %collective-permute-start.6 = (bf16[2,512,768]{2,1,0:T(8,128)(2,1)}, bf16[2,512,768]{2,1,0:T(8,128)(2,1)S(1)}, u32[]{:S(2)}, u32[]{:S(2)}) collective-permute-start(bf16[2,512,768]{2,1,0:T(8,128)(2,1)} %get-tuple-element.70.refs_8_), channel_id=1, source_target_pairs={{0,16},{16,0},{1,17},{17,1},{2,18},{18,2},{3,19},{19,3},{4,20},{20... | collective-permute-start | bytes 4718600 | tf_op jit(solution)/shard_map/ppermute | solution.py:1058
  150.1 0.1 collective-permute-start.7
  150.2 3.8 %collective-permute-done.7 = bf16[4,72,768]{2,1,0:T(8,128)(2,1)S(1)} collective-permute-done((bf16[4,72,768]{2,1,0:T(8,128)(2,1)}, bf16[4,72,768]{2,1,0:T(8,128)(2,1)S(1)}, u32[]{:S(2)}, u32[]{:S(2)}) %collective-permute-start.7) | collective-permute-done | bytes 442400 | tf_op jit(solution)/shard_map/ppermute | solution.py:1058
  154.0 1.1 add.31
  155.2 3.7 %collective-permute-start.10 = (bf16[72,768]{1,0:T(8,128)(2,1)S(1)}, bf16[72,768]{1,0:T(8,128)(2,1)S(1)}, u32[]{:S(2)}, u32[]{:S(2)}) collective-permute-start(bf16[72,768]{1,0:T(8,128)(2,1)S(1)} %get-tuple-element.92), channel_id=1, source_target_pairs={{0,3},{1,2},{2,1},{3,0},{4,7},{5,6},{6,5},{7,4},{8,11},{9,10},{10,... | collective-permute-start | bytes 331784 | tf_op jit(solution)/shard_map/ppermute | solution.py:1067
  158.8 0.5 collective-permute-start.8
  159.4 0.1 collective-permute-start.9
  159.5 3.3 %collective-permute-done.10 = bf16[72,768]{1,0:T(8,128)(2,1)S(1)} collective-permute-done((bf16[72,768]{1,0:T(8,128)(2,1)S(1)}, bf16[72,768]{1,0:T(8,128)(2,1)S(1)}, u32[]{:S(2)}, u32[]{:S(2)}) %collective-permute-start.10) | collective-permute-done | bytes 110624 | tf_op jit(solution)/shard_map/ppermute | solution.py:1067
  162.7 2.3 %collective-permute-done.8 = bf16[72,768]{1,0:T(8,128)(2,1)S(1)} collective-permute-done((bf16[72,768]{1,0:T(8,128)(2,1)S(1)}, bf16[72,768]{1,0:T(8,128)(2,1)S(1)}, u32[]{:S(2)}, u32[]{:S(2)}) %collective-permute-start.8) | collective-permute-done | bytes 110624 | tf_op jit(solution)/shard_map/ppermute | solution.py:1067
  165.0 0.0 collective-permute-done.9
  165.0 0.1 fusion.1
  165.1 1.6 collective-permute-start.11
  166.7 3.2 %collective-permute-done.11 = bf16[72,768]{1,0:T(8,128)(2,1)S(1)} collective-permute-done((bf16[72,768]{1,0:T(8,128)(2,1)S(1)}, bf16[72,768]{1,0:T(8,128)(2,1)S(1)}, u32[]{:S(2)}, u32[]{:S(2)}) %collective-permute-start.11) | collective-permute-done | bytes 110624 | tf_op jit(solution)/shard_map/ppermute | solution.py:1067
  169.9 2.6 %collective-permute-start.12 = (bf16[72,768]{1,0:T(8,128)(2,1)S(1)}, bf16[72,768]{1,0:T(8,128)(2,1)S(1)}, u32[]{:S(2)}, u32[]{:S(2)}) collective-permute-start(bf16[72,768]{1,0:T(8,128)(2,1)S(1)} %add.39), channel_id=1, source_target_pairs={{0,8},{1,9},{2,10},{3,11},{4,12},{5,13},{6,14},{7,15},{8,0},{9,1},... | collective-permute-start | bytes 331784 | tf_op jit(solution)/shard_map/ppermute | solution.py:1067
  172.6 4.2 %collective-permute-done.12 = bf16[72,768]{1,0:T(8,128)(2,1)S(1)} collective-permute-done((bf16[72,768]{1,0:T(8,128)(2,1)S(1)}, bf16[72,768]{1,0:T(8,128)(2,1)S(1)}, u32[]{:S(2)}, u32[]{:S(2)}) %collective-permute-start.12) | collective-permute-done | bytes 110624 | tf_op jit(solution)/shard_map/ppermute | solution.py:1067
  176.9 3.2 %collective-permute-start.15 = (bf16[72,768]{1,0:T(8,128)(2,1)S(1)}, bf16[72,768]{1,0:T(8,128)(2,1)S(1)}, u32[]{:S(2)}, u32[]{:S(2)}) collective-permute-start(bf16[72,768]{1,0:T(8,128)(2,1)S(1)} %add.40.refs_0_), channel_id=1, source_target_pairs={{0,3},{1,2},{2,1},{3,0},{4,7},{5,6},{6,5},{7,4},{8,11},{9,10},{10,... | collective-permute-start | bytes 331784 | tf_op jit(solution)/shard_map/ppermute | solution.py:1067
  180.1 0.0 collective-permute-start.14
  180.1 0.6 collective-permute-start.13
  180.8 0.0 collective-permute-done.6.refs_9_
  180.8 0.0 copy-start.1
  180.8 1.2 copy-done.1
  181.9 25.5 %attn_back.1 = (bf16[2,512,768]{2,1,0:T(8,128)(2,1)}, bf16[4,512,768]{2,1,0:T(8,128)(2,1)}) custom-call(s32[1]{0:T(128)} %bitcast.section, bf16[2,512,2304]{2,1,0:T(8,128)(2,1)} %get-tuple-element.55.refs_0_, bf16[2,512,768]{2,1,0:T(8,128)(2,1)} %get-tuple-element.65.refs_1_, bf16[2,512,768]{2,1,0:T(8,128)(2,1)} %get-tuple-element.66.refs_2_, ...), custom_call_target="tpu_custom_call" | custom-call | flops 14495514624 | bytes 1048576 | tf_op jit(solution)/shard_map/attn_back/pallas_call | solution.py:494
  207.5 0.0 collective-permute-done.15.refs_3_
  207.5 0.0 collective-permute-done.14.refs_2_
  207.5 0.0 collective-permute-done.13.refs_1_
  207.5 1.0 unpack.1
  (3 shorter events, 0.1 us)
Async XLA Ops:
  0.6 8.9 %collective-permute-start = (bf16[1,768,2304]{2,1,0:T(8,128)(2,1)}, bf16[1,768,2304]{2,1,0:T(8,128)(2,1)S(1)}, u32[]{:S(2)}, u32[]{:S(2)}) collective-permute-start(bf16[1,768,2304]{2,1,0:T(8,128)(2,1)} %refs_6_.3), channel_id=1, source_target_pairs={{0,16},{16,0},{1,17},{17,1},{2,18},{18,2},{3,19},{19,3},{4,20},{20... | collective-permute-start | bytes 10616840 | tf_op jit(solution)/shard_map/ppermute | solution.py:1058
  1.2 8.4 %collective-permute-start.1 = (bf16[1,768,768]{2,1,0:T(8,128)(2,1)}, bf16[1,768,768]{2,1,0:T(8,128)(2,1)}, u32[]{:S(2)}, u32[]{:S(2)}) collective-permute-start(bf16[1,768,768]{2,1,0:T(8,128)(2,1)} %refs_11_.3), channel_id=1, source_target_pairs={{0,16},{16,0},{1,17},{17,1},{2,18},{18,2},{3,19},{19,3},{4,20},{20... | collective-permute-start | bytes 3538952 | tf_op jit(solution)/shard_map/ppermute | solution.py:1058
  3.1 6.4 %collective-permute-start.2 = (bf16[4,64,768]{2,1,0:T(8,128)(2,1)}, bf16[4,64,768]{2,1,0:T(8,128)(2,1)S(1)}, u32[]{:S(2)}, u32[]{:S(2)}) collective-permute-start(bf16[4,64,768]{2,1,0:T(8,128)(2,1)} %get-tuple-element.53.refs_6_.refs_17_), channel_id=1, source_target_pairs={{0,16},{16,0},{1,17},{17,1},{2,18},{18,2},{3,19},{19,3},{4,20},{20... | collective-permute-start | bytes 1179656 | tf_op jit(solution)/shard_map/ppermute | solution.py:1058
  3.6 5.9 %collective-permute-start.3 = (f32[2,4,768]{2,1,0:T(4,128)}, f32[2,4,768]{2,1,0:T(4,128)S(1)}, u32[]{:S(2)}, u32[]{:S(2)}) collective-permute-start(f32[2,4,768]{2,1,0:T(4,128)} %get-tuple-element.54.refs_8_.refs_19_), channel_id=1, source_target_pairs={{0,16},{16,0},{1,17},{17,1},{2,18},{18,2},{3,19},{19,3},{4,20},{20... | collective-permute-start | bytes 73736 | tf_op jit(solution)/shard_map/ppermute | solution.py:1058
  9.5 1.2 copy-start.3
  9.5 0.8 copy-start.2
  10.3 1.9 copy-start
  10.3 22.5 %collective-permute-start.4 = (bf16[1,768,3072]{2,1,0:T(8,128)(2,1)}, bf16[1,768,3072]{2,1,0:T(8,128)(2,1)}, u32[]{:S(2)}, u32[]{:S(2)}) collective-permute-start(bf16[1,768,3072]{2,1,0:T(8,128)(2,1)} %refs_13_.1), channel_id=1, source_target_pairs={{0,16},{16,0},{1,17},{17,1},{2,18},{18,2},{3,19},{19,3},{4,20},{20... | collective-permute-start | bytes 14155784 | tf_op jit(solution)/shard_map/ppermute | solution.py:1058
  10.7 22.1 %collective-permute-start.5 = (bf16[1,3072,768]{2,1,0:T(8,128)(2,1)}, bf16[1,3072,768]{2,1,0:T(8,128)(2,1)}, u32[]{:S(2)}, u32[]{:S(2)}) collective-permute-start(bf16[1,3072,768]{2,1,0:T(8,128)(2,1)} %refs_15_.1), channel_id=1, source_target_pairs={{0,16},{16,0},{1,17},{17,1},{2,18},{18,2},{3,19},{19,3},{4,20},{20... | collective-permute-start | bytes 14155784 | tf_op jit(solution)/shard_map/ppermute | solution.py:1058
  145.0 35.8 %collective-permute-start.6 = (bf16[2,512,768]{2,1,0:T(8,128)(2,1)}, bf16[2,512,768]{2,1,0:T(8,128)(2,1)S(1)}, u32[]{:S(2)}, u32[]{:S(2)}) collective-permute-start(bf16[2,512,768]{2,1,0:T(8,128)(2,1)} %get-tuple-element.70.refs_8_), channel_id=1, source_target_pairs={{0,16},{16,0},{1,17},{17,1},{2,18},{18,2},{3,19},{19,3},{4,20},{20... | collective-permute-start | bytes 4718600 | tf_op jit(solution)/shard_map/ppermute | solution.py:1058
  150.1 3.9 %collective-permute-start.7 = (bf16[4,72,768]{2,1,0:T(8,128)(2,1)}, bf16[4,72,768]{2,1,0:T(8,128)(2,1)S(1)}, u32[]{:S(2)}, u32[]{:S(2)}) collective-permute-start(bf16[4,72,768]{2,1,0:T(8,128)(2,1)} %get-tuple-element.74), channel_id=1, source_target_pairs={{0,16},{16,0},{1,17},{17,1},{2,18},{18,2},{3,19},{19,3},{4,20},{20... | collective-permute-start | bytes 1327112 | tf_op jit(solution)/shard_map/ppermute | solution.py:1058
  155.2 7.5 %collective-permute-start.10 = (bf16[72,768]{1,0:T(8,128)(2,1)S(1)}, bf16[72,768]{1,0:T(8,128)(2,1)S(1)}, u32[]{:S(2)}, u32[]{:S(2)}) collective-permute-start(bf16[72,768]{1,0:T(8,128)(2,1)S(1)} %get-tuple-element.92), channel_id=1, source_target_pairs={{0,3},{1,2},{2,1},{3,0},{4,7},{5,6},{6,5},{7,4},{8,11},{9,10},{10,... | collective-permute-start | bytes 331784 | tf_op jit(solution)/shard_map/ppermute | solution.py:1067
  158.8 6.2 %collective-permute-start.8 = (bf16[72,768]{1,0:T(8,128)(2,1)S(1)}, bf16[72,768]{1,0:T(8,128)(2,1)S(1)}, u32[]{:S(2)}, u32[]{:S(2)}) collective-permute-start(bf16[72,768]{1,0:T(8,128)(2,1)S(1)} %get-tuple-element.91), channel_id=1, source_target_pairs={{0,1},{1,0},{2,3},{3,2},{4,5},{5,4},{6,7},{7,6},{8,9},{9,8},{10,11... | collective-permute-start | bytes 331784 | tf_op jit(solution)/shard_map/ppermute | solution.py:1067
  159.4 5.7 %collective-permute-start.9 = (bf16[72,768]{1,0:T(8,128)(2,1)S(1)}, bf16[72,768]{1,0:T(8,128)(2,1)S(1)}, u32[]{:S(2)}, u32[]{:S(2)}) collective-permute-start(bf16[72,768]{1,0:T(8,128)(2,1)S(1)} %get-tuple-element.93), channel_id=1, source_target_pairs={{0,2},{1,3},{2,0},{3,1},{4,6},{5,7},{6,4},{7,5},{8,10},{9,11},{10,... | collective-permute-start | bytes 331784 | tf_op jit(solution)/shard_map/ppermute | solution.py:1067
  165.1 4.8 %collective-permute-start.11 = (bf16[72,768]{1,0:T(8,128)(2,1)S(1)}, bf16[72,768]{1,0:T(8,128)(2,1)S(1)}, u32[]{:S(2)}, u32[]{:S(2)}) collective-permute-start(bf16[72,768]{1,0:T(8,128)(2,1)S(1)} %fusion.1), channel_id=1, source_target_pairs={{0,4},{1,5},{2,6},{3,7},{4,0},{5,1},{6,2},{7,3},{8,12},{9,13},{10,... | collective-permute-start | bytes 331784 | tf_op jit(solution)/shard_map/ppermute | solution.py:1067
  169.9 6.9 %collective-permute-start.12 = (bf16[72,768]{1,0:T(8,128)(2,1)S(1)}, bf16[72,768]{1,0:T(8,128)(2,1)S(1)}, u32[]{:S(2)}, u32[]{:S(2)}) collective-permute-start(bf16[72,768]{1,0:T(8,128)(2,1)S(1)} %add.39), channel_id=1, source_target_pairs={{0,8},{1,9},{2,10},{3,11},{4,12},{5,13},{6,14},{7,15},{8,0},{9,1},... | collective-permute-start | bytes 331784 | tf_op jit(solution)/shard_map/ppermute | solution.py:1067
  176.9 30.6 %collective-permute-start.15 = (bf16[72,768]{1,0:T(8,128)(2,1)S(1)}, bf16[72,768]{1,0:T(8,128)(2,1)S(1)}, u32[]{:S(2)}, u32[]{:S(2)}) collective-permute-start(bf16[72,768]{1,0:T(8,128)(2,1)S(1)} %add.40.refs_0_), channel_id=1, source_target_pairs={{0,3},{1,2},{2,1},{3,0},{4,7},{5,6},{6,5},{7,4},{8,11},{9,10},{10,... | collective-permute-start | bytes 331784 | tf_op jit(solution)/shard_map/ppermute | solution.py:1067
  180.1 27.4 %collective-permute-start.14 = (bf16[72,768]{1,0:T(8,128)(2,1)S(1)}, bf16[72,768]{1,0:T(8,128)(2,1)S(1)}, u32[]{:S(2)}, u32[]{:S(2)}) collective-permute-start(bf16[72,768]{1,0:T(8,128)(2,1)S(1)} %add.40.refs_0_), channel_id=1, source_target_pairs={{0,2},{1,3},{2,0},{3,1},{4,6},{5,7},{6,4},{7,5},{8,10},{9,11},{10,... | collective-permute-start | bytes 331784 | tf_op jit(solution)/shard_map/ppermute | solution.py:1067
  180.1 27.4 %collective-permute-start.13 = (bf16[72,768]{1,0:T(8,128)(2,1)S(1)}, bf16[72,768]{1,0:T(8,128)(2,1)S(1)}, u32[]{:S(2)}, u32[]{:S(2)}) collective-permute-start(bf16[72,768]{1,0:T(8,128)(2,1)S(1)} %add.40.refs_0_), channel_id=1, source_target_pairs={{0,1},{1,0},{2,3},{3,2},{4,5},{5,4},{6,7},{7,6},{8,9},{9,8},{10,11... | collective-permute-start | bytes 331784 | tf_op jit(solution)/shard_map/ppermute | solution.py:1067
  180.8 1.2 copy-start.1

commit v2 on v1

--- a/solution.py
+++ b/solution.py
@@ -1005,6 +1005,7 @@
             jax.ShapeDtypeStruct((4, 64, width), BF),
             jax.ShapeDtypeStruct((2, 4, width), F32),
         ),
+        compiler_params=pltpu.CompilerParams(vmem_limit_bytes=62 << 20),
         name="pack",
     )(*mats, *vecs)
 
@@ -1067,12 +1068,13 @@
     return lax.ppermute(value, "dp", [(at, at ^ bits) for at in range(count)])
 
 
-def summed_quarters(part):
+def summed_quarters(parts, before_last):
     mine, count = lax.axis_index("dp"), lax.axis_size("dp")
     member = mine & 3
 
     def quarter(d):
-        return lax.dynamic_index_in_dim(part, member ^ d, 0, keepdims=False)
+        first, second = (lax.dynamic_index_in_dim(v, member ^ d, 0, keepdims=False) for v in parts)
+        return first + second
 
     def together(own, a, b, c):
         own, a, b, c = (v.astype(F32) for v in (own, a, b, c))
@@ -1083,6 +1085,7 @@
     while bit < count:
         total = total + exchanged(total, bit)
         bit *= 2
+    total = after(total, before_last)
     return [total] + [exchanged(total, d) for d in (1, 2, 3)], member
 
 
@@ -1108,9 +1111,10 @@
 
     kept = first_attn_forward(where, tokens, valid, own, got, sizes, slots)
     back = middle_part(where, kept, cotangent, valid, own, got, sizes, slots)
-    there = swap(back.result)
-
-    quarters, member = summed_quarters(back.keep + swap(back.send))
+
+    got_grads = swap(back.send)
+    there = swap(after(back.result, got_grads))
+    quarters, member = summed_quarters((back.keep, got_grads), there)
     last = first_attn_backward(where, back, there, kept, own, got, sizes, slots)
     small = unpacked([quarters[0]] + [after(v, last.input_grad) for v in quarters[1:]], member)
     return (last.result, last.input_grad) + small

time: 209 us -> 205 us (0.981)
  local copies, waits for them, and re-layouts: 3.33 us -> 0.46 us
  waiting for transfers between devices: 22.7 us -> 20.4 us
    unnamed x8, local copies, waits for them, and re-layouts: 3.29 us -> 0.46 us
    ppermute x8, waiting for transfers between devices: 9.72 us -> 7.61 us  [swap(): return lax.ppermute(value, 'section', [(0, 1), (1, 0)])]
  transfers between devices with their start and end apart: 16 -> 16, of which waited for: 6 -> 7; matrix products, arithmetic and copies ran while one was open for 1% -> 1% of each run, Pallas kernels for 23% -> 23%
where the time goes in v2:
time: 205 us; the launch traced here: 204 us
  Pallas kernels  161 us (79%)
  waiting for transfers between devices  20.4 us (10%)
  starting transfers between devices  19.5 us (10%)
  other arithmetic  2.09 us (1%)
    pallas_call x3, Pallas kernels, run(): pl.pallas_call(kernel, out_shape=self.outs, grid_spec=pltpu.PrefetchScala...  158 us
    ppermute x8, waiting for transfers between devices, exchanged(): return lax.ppermute(value, 'dp', [(at, at ^ bits) for at in range(count)])  12.7 us
    ppermute x8, starting transfers between devices, exchanged(): return lax.ppermute(value, 'dp', [(at, at ^ bits) for at in range(count)])  12.6 us
    ppermute x8, waiting for transfers between devices, swap(): return lax.ppermute(value, 'section', [(0, 1), (1, 0)])  7.61 us
    ppermute x8, starting transfers between devices, swap(): return lax.ppermute(value, 'section', [(0, 1), (1, 0)])  6.9 us
  transfers between devices with their start and end apart: 16, of which 7 were waited for; matrix products, arithmetic and copies ran while one was open for 1% of the time, Pallas kernels for 23%

profile of v2, /device:TPU:0, one launch (start us, length us, event | category | flops | bytes accessed | tf_op | source)
XLA Modules:
  0.0 204.4 jit_solution(14764625147392259894)
XLA Ops:
  0.6 0.5 collective-permute-start
  1.2 0.1 collective-permute-start.1
  1.2 1.9 pack.1
  3.1 0.4 collective-permute-start.2
  3.6 0.1 collective-permute-start.3
  3.7 5.8 %collective-permute-done.3.refs_9_.refs_20_ = f32[2,4,768]{2,1,0:T(4,128)S(1)} collective-permute-done((f32[2,4,768]{2,1,0:T(4,128)}, f32[2,4,768]{2,1,0:T(4,128)S(1)}, u32[]{:S(2)}, u32[]{:S(2)}) %collective-permute-start.3) | collective-permute-done | bytes 24608 | tf_op jit(solution)/shard_map/ppermute | solution.py:1059
  9.4 0.0 copy-start.3
  9.4 0.0 collective-permute-done.2.refs_7_.refs_18_
  9.4 0.0 copy-start.2
  9.4 0.0 collective-permute-done.1.refs_5_.refs_12_
  9.4 0.0 copy-start.1
  9.5 0.2 collective-permute-done.refs_3_.refs_10_.refs_7_
  9.6 0.4 collective-permute-start.4
  10.0 0.1 collective-permute-start.5
  10.2 0.0 copy-done.3
  10.2 0.1 copy-done.2
  10.2 0.4 copy-done.1
  10.6 20.6 %first_attn.1 = (bf16[2,512,2304]{2,1,0:T(8,128)(2,1)}, bf16[2,512,768]{2,1,0:T(8,128)(2,1)}, bf16[2,512,768]{2,1,0:T(8,128)(2,1)}, bf16[2,512,768]{2,1,0:T(8,12...) custom-call(s32[1]{0:T(128)} %bitcast.section, ...), custom_call_target="tpu_custom_call" | custom-call | flops 14495514624 | bytes 1048576 | tf_op jit(solution)/shard_map/first_attn/pallas_call | solution.py:494
  31.2 0.0 collective-permute-done.4.refs_14_
  31.2 0.0 collective-permute-done.5.refs_16_
  31.2 112.1 %middle_part.1 = (bf16[2,512,768]{2,1,0:T(8,128)(2,1)}, bf16[2,512,768]{2,1,0:T(8,128)(2,1)}, bf16[2,512,768]{2,1,0:T(8,128)(2,1)}, bf16[4,72,768]{2,1,0:T(8,128)(2,1)}, bf16[4,72,768]{2,1,0:T(8,128)(2,1)}) custom-call(s32[1]{0:T(128)} %bitcast.section, bf16[2,512,768]{2,1,0:T(8,128)(2,1)} %get-tuple-element.58.refs_0_, bf16[4,512,768]{2,1,0:T(8,128)(2,1)} %refs_1_.5, ...), custom_call_target="tpu_custom_call" | custom-call | flops 86973087744 | bytes 1048576 | tf_op jit(solution)/shard_map/middle_part/pallas_call | solution.py:494
  143.4 4.9 %collective-permute-start.6 = (bf16[4,72,768]{2,1,0:T(8,128)(2,1)}, bf16[4,72,768]{2,1,0:T(8,128)(2,1)S(1)}, u32[]{:S(2)}, u32[]{:S(2)}) collective-permute-start(bf16[4,72,768]{2,1,0:T(8,128)(2,1)} %get-tuple-element.73), channel_id=1, source_target_pairs={{0,16},{16,0},{1,17},{17,1},{2,18},{18,2},{3,19},{19,3},{4,20},{20... | collective-permute-start | bytes 1327112 | tf_op jit(solution)/shard_map/ppermute | solution.py:1059
  148.3 1.6 collective-permute-done.6
  149.9 0.4 collective-permute-start.7
  150.3 1.0 add_bitcast_fusion.2
  151.4 3.8 %collective-permute-start.10 = (bf16[72,768]{1,0:T(8,128)(2,1)S(1)}, bf16[72,768]{1,0:T(8,128)(2,1)S(1)}, u32[]{:S(2)}, u32[]{:S(2)}) collective-permute-start(bf16[72,768]{1,0:T(8,128)(2,1)S(1)} %get-tuple-element.96), channel_id=1, source_target_pairs={{0,3},{1,2},{2,1},{3,0},{4,7},{5,6},{6,5},{7,4},{8,11},{9,10},{10,... | collective-permute-start | bytes 331784 | tf_op jit(solution)/shard_map/ppermute | solution.py:1068
  155.2 0.5 collective-permute-start.8
  155.7 0.1 collective-permute-start.9
  155.8 3.2 %collective-permute-done.10 = bf16[72,768]{1,0:T(8,128)(2,1)S(1)} collective-permute-done((bf16[72,768]{1,0:T(8,128)(2,1)S(1)}, bf16[72,768]{1,0:T(8,128)(2,1)S(1)}, u32[]{:S(2)}, u32[]{:S(2)}) %collective-permute-start.10) | collective-permute-done | bytes 110624 | tf_op jit(solution)/shard_map/ppermute | solution.py:1068
  159.0 2.1 %collective-permute-done.8 = bf16[72,768]{1,0:T(8,128)(2,1)S(1)} collective-permute-done((bf16[72,768]{1,0:T(8,128)(2,1)S(1)}, bf16[72,768]{1,0:T(8,128)(2,1)S(1)}, u32[]{:S(2)}, u32[]{:S(2)}) %collective-permute-start.8) | collective-permute-done | bytes 110624 | tf_op jit(solution)/shard_map/ppermute | solution.py:1068
  161.2 0.0 collective-permute-done.9
  161.2 1.0 fusion.1
  162.2 1.6 collective-permute-start.11
  163.8 3.2 %collective-permute-done.11 = bf16[72,768]{1,0:T(8,128)(2,1)S(1)} collective-permute-done((bf16[72,768]{1,0:T(8,128)(2,1)S(1)}, bf16[72,768]{1,0:T(8,128)(2,1)S(1)}, u32[]{:S(2)}, u32[]{:S(2)}) %collective-permute-start.11) | collective-permute-done | bytes 110624 | tf_op jit(solution)/shard_map/ppermute | solution.py:1068
  167.0 2.7 %collective-permute-start.12 = (bf16[72,768]{1,0:T(8,128)(2,1)S(1)}, bf16[72,768]{1,0:T(8,128)(2,1)S(1)}, u32[]{:S(2)}, u32[]{:S(2)}) collective-permute-start(bf16[72,768]{1,0:T(8,128)(2,1)S(1)} %add.68), channel_id=1, source_target_pairs={{0,8},{1,9},{2,10},{3,11},{4,12},{5,13},{6,14},{7,15},{8,0},{9,1},... | collective-permute-start | bytes 331784 | tf_op jit(solution)/shard_map/ppermute | solution.py:1068
  169.7 4.2 %collective-permute-done.12 = bf16[72,768]{1,0:T(8,128)(2,1)S(1)} collective-permute-done((bf16[72,768]{1,0:T(8,128)(2,1)S(1)}, bf16[72,768]{1,0:T(8,128)(2,1)S(1)}, u32[]{:S(2)}, u32[]{:S(2)}) %collective-permute-start.12) | collective-permute-done | bytes 110624 | tf_op jit(solution)/shard_map/ppermute | solution.py:1068
  173.9 0.0 collective-permute-done.7.refs_9_
  173.9 0.0 copy-start
  174.0 3.1 %collective-permute-start.15 = (bf16[72,768]{1,0:T(8,128)(2,1)S(1)}, bf16[72,768]{1,0:T(8,128)(2,1)S(1)}, u32[]{:S(2)}, u32[]{:S(2)}) collective-permute-start(bf16[72,768]{1,0:T(8,128)(2,1)S(1)} %add.69.refs_0_), channel_id=1, source_target_pairs={{0,3},{1,2},{2,1},{3,0},{4,7},{5,6},{6,5},{7,4},{8,11},{9,10},{10,... | collective-permute-start | bytes 331784 | tf_op jit(solution)/shard_map/ppermute | solution.py:1068
  177.1 0.0 collective-permute-start.14
  177.1 0.7 collective-permute-start.13
  177.8 0.0 copy-done
  177.8 25.5 %attn_back.1 = (bf16[2,512,768]{2,1,0:T(8,128)(2,1)}, bf16[4,512,768]{2,1,0:T(8,128)(2,1)}) custom-call(s32[1]{0:T(128)} %bitcast.section, bf16[2,512,2304]{2,1,0:T(8,128)(2,1)} %get-tuple-element.57.refs_0_, bf16[2,512,768]{2,1,0:T(8,128)(2,1)} %get-tuple-element.67.refs_1_, bf16[2,512,768]{2,1,0:T(8,128)(2,1)} %get-tuple-element.68.refs_2_, ...), custom_call_target="tpu_custom_call" | custom-call | flops 14495514624 | bytes 1048576 | tf_op jit(solution)/shard_map/attn_back/pallas_call | solution.py:494
  203.3 0.0 collective-permute-done.15.refs_3_
  203.3 0.0 collective-permute-done.14.refs_2_
  203.3 0.0 collective-permute-done.13.refs_1_
  203.3 1.0 unpack.1
  (2 shorter events, 0.1 us)
Async XLA Ops:
  0.6 9.0 %collective-permute-start = (bf16[1,768,2304]{2,1,0:T(8,128)(2,1)}, bf16[1,768,2304]{2,1,0:T(8,128)(2,1)}, u32[]{:S(2)}, u32[]{:S(2)}) collective-permute-start(bf16[1,768,2304]{2,1,0:T(8,128)(2,1)} %refs_6_.3), channel_id=1, source_target_pairs={{0,16},{16,0},{1,17},{17,1},{2,18},{18,2},{3,19},{19,3},{4,20},{20... | collective-permute-start | bytes 10616840 | tf_op jit(solution)/shard_map/ppermute | solution.py:1059
  1.2 8.3 %collective-permute-start.1 = (bf16[1,768,768]{2,1,0:T(8,128)(2,1)}, bf16[1,768,768]{2,1,0:T(8,128)(2,1)S(1)}, u32[]{:S(2)}, u32[]{:S(2)}) collective-permute-start(bf16[1,768,768]{2,1,0:T(8,128)(2,1)} %refs_11_.3), channel_id=1, source_target_pairs={{0,16},{16,0},{1,17},{17,1},{2,18},{18,2},{3,19},{19,3},{4,20},{20... | collective-permute-start | bytes 3538952 | tf_op jit(solution)/shard_map/ppermute | solution.py:1059
  3.1 6.3 %collective-permute-start.2 = (bf16[4,64,768]{2,1,0:T(8,128)(2,1)}, bf16[4,64,768]{2,1,0:T(8,128)(2,1)S(1)}, u32[]{:S(2)}, u32[]{:S(2)}) collective-permute-start(bf16[4,64,768]{2,1,0:T(8,128)(2,1)} %get-tuple-element.55.refs_6_.refs_17_), channel_id=1, source_target_pairs={{0,16},{16,0},{1,17},{17,1},{2,18},{18,2},{3,19},{19,3},{4,20},{20... | collective-permute-start | bytes 1179656 | tf_op jit(solution)/shard_map/ppermute | solution.py:1059
  3.6 5.9 %collective-permute-start.3 = (f32[2,4,768]{2,1,0:T(4,128)}, f32[2,4,768]{2,1,0:T(4,128)S(1)}, u32[]{:S(2)}, u32[]{:S(2)}) collective-permute-start(f32[2,4,768]{2,1,0:T(4,128)} %get-tuple-element.56.refs_8_.refs_19_), channel_id=1, source_target_pairs={{0,16},{16,0},{1,17},{17,1},{2,18},{18,2},{3,19},{19,3},{4,20},{20... | collective-permute-start | bytes 73736 | tf_op jit(solution)/shard_map/ppermute | solution.py:1059
  9.4 0.7 copy-start.3
  9.4 0.8 copy-start.2
  9.4 1.2 copy-start.1
  9.6 21.6 %collective-permute-start.4 = (bf16[1,768,3072]{2,1,0:T(8,128)(2,1)}, bf16[1,768,3072]{2,1,0:T(8,128)(2,1)}, u32[]{:S(2)}, u32[]{:S(2)}) collective-permute-start(bf16[1,768,3072]{2,1,0:T(8,128)(2,1)} %refs_13_.1), channel_id=1, source_target_pairs={{0,16},{16,0},{1,17},{17,1},{2,18},{18,2},{3,19},{19,3},{4,20},{20... | collective-permute-start | bytes 14155784 | tf_op jit(solution)/shard_map/ppermute | solution.py:1059
  10.0 21.2 %collective-permute-start.5 = (bf16[1,3072,768]{2,1,0:T(8,128)(2,1)}, bf16[1,3072,768]{2,1,0:T(8,128)(2,1)}, u32[]{:S(2)}, u32[]{:S(2)}) collective-permute-start(bf16[1,3072,768]{2,1,0:T(8,128)(2,1)} %refs_15_.1), channel_id=1, source_target_pairs={{0,16},{16,0},{1,17},{17,1},{2,18},{18,2},{3,19},{19,3},{4,20},{20... | collective-permute-start | bytes 14155784 | tf_op jit(solution)/shard_map/ppermute | solution.py:1059
  143.4 6.5 %collective-permute-start.6 = (bf16[4,72,768]{2,1,0:T(8,128)(2,1)}, bf16[4,72,768]{2,1,0:T(8,128)(2,1)S(1)}, u32[]{:S(2)}, u32[]{:S(2)}) collective-permute-start(bf16[4,72,768]{2,1,0:T(8,128)(2,1)} %get-tuple-element.73), channel_id=1, source_target_pairs={{0,16},{16,0},{1,17},{17,1},{2,18},{18,2},{3,19},{19,3},{4,20},{20... | collective-permute-start | bytes 1327112 | tf_op jit(solution)/shard_map/ppermute | solution.py:1059
  149.9 24.0 %collective-permute-start.7 = (bf16[2,512,768]{2,1,0:T(8,128)(2,1)}, bf16[2,512,768]{2,1,0:T(8,128)(2,1)S(1)}, u32[]{:S(2)}, u32[]{:S(2)}) collective-permute-start(bf16[2,512,768]{2,1,0:T(8,128)(2,1)} %get-tuple-element.74.refs_8_), channel_id=1, source_target_pairs={{0,16},{16,0},{1,17},{17,1},{2,18},{18,2},{3,19},{19,3},{4,20},{20... | collective-permute-start | bytes 4718600 | tf_op jit(solution)/shard_map/ppermute | solution.py:1059
  151.4 7.7 %collective-permute-start.10 = (bf16[72,768]{1,0:T(8,128)(2,1)S(1)}, bf16[72,768]{1,0:T(8,128)(2,1)S(1)}, u32[]{:S(2)}, u32[]{:S(2)}) collective-permute-start(bf16[72,768]{1,0:T(8,128)(2,1)S(1)} %get-tuple-element.96), channel_id=1, source_target_pairs={{0,3},{1,2},{2,1},{3,0},{4,7},{5,6},{6,5},{7,4},{8,11},{9,10},{10,... | collective-permute-start | bytes 331784 | tf_op jit(solution)/shard_map/ppermute | solution.py:1068
  155.2 6.0 %collective-permute-start.8 = (bf16[72,768]{1,0:T(8,128)(2,1)S(1)}, bf16[72,768]{1,0:T(8,128)(2,1)S(1)}, u32[]{:S(2)}, u32[]{:S(2)}) collective-permute-start(bf16[72,768]{1,0:T(8,128)(2,1)S(1)} %get-tuple-element.95), channel_id=1, source_target_pairs={{0,1},{1,0},{2,3},{3,2},{4,5},{5,4},{6,7},{7,6},{8,9},{9,8},{10,11... | collective-permute-start | bytes 331784 | tf_op jit(solution)/shard_map/ppermute | solution.py:1068
  155.7 5.4 %collective-permute-start.9 = (bf16[72,768]{1,0:T(8,128)(2,1)S(1)}, bf16[72,768]{1,0:T(8,128)(2,1)S(1)}, u32[]{:S(2)}, u32[]{:S(2)}) collective-permute-start(bf16[72,768]{1,0:T(8,128)(2,1)S(1)} %get-tuple-element.97), channel_id=1, source_target_pairs={{0,2},{1,3},{2,0},{3,1},{4,6},{5,7},{6,4},{7,5},{8,10},{9,11},{10,... | collective-permute-start | bytes 331784 | tf_op jit(solution)/shard_map/ppermute | solution.py:1068
  162.2 4.8 %collective-permute-start.11 = (bf16[72,768]{1,0:T(8,128)(2,1)S(1)}, bf16[72,768]{1,0:T(8,128)(2,1)S(1)}, u32[]{:S(2)}, u32[]{:S(2)}) collective-permute-start(bf16[72,768]{1,0:T(8,128)(2,1)S(1)} %fusion.1), channel_id=1, source_target_pairs={{0,4},{1,5},{2,6},{3,7},{4,0},{5,1},{6,2},{7,3},{8,12},{9,13},{10,... | collective-permute-start | bytes 331784 | tf_op jit(solution)/shard_map/ppermute | solution.py:1068
  167.0 6.9 %collective-permute-start.12 = (bf16[72,768]{1,0:T(8,128)(2,1)S(1)}, bf16[72,768]{1,0:T(8,128)(2,1)S(1)}, u32[]{:S(2)}, u32[]{:S(2)}) collective-permute-start(bf16[72,768]{1,0:T(8,128)(2,1)S(1)} %add.68), channel_id=1, source_target_pairs={{0,8},{1,9},{2,10},{3,11},{4,12},{5,13},{6,14},{7,15},{8,0},{9,1},... | collective-permute-start | bytes 331784 | tf_op jit(solution)/shard_map/ppermute | solution.py:1068
  173.9 3.8 %copy-start = (bf16[2,512,768]{2,1,0:T(8,128)(2,1)}, bf16[2,512,768]{2,1,0:T(8,128)(2,1)S(1)}, u32[]{:S(2)}) copy-start(bf16[2,512,768]{2,1,0:T(8,128)(2,1)S(1)} %collective-permute-done.7.refs_9_) | copy-start | bytes 4718596
  174.0 29.3 %collective-permute-start.15 = (bf16[72,768]{1,0:T(8,128)(2,1)S(1)}, bf16[72,768]{1,0:T(8,128)(2,1)S(1)}, u32[]{:S(2)}, u32[]{:S(2)}) collective-permute-start(bf16[72,768]{1,0:T(8,128)(2,1)S(1)} %add.69.refs_0_), channel_id=1, source_target_pairs={{0,3},{1,2},{2,1},{3,0},{4,7},{5,6},{6,5},{7,4},{8,11},{9,10},{10,... | collective-permute-start | bytes 331784 | tf_op jit(solution)/shard_map/ppermute | solution.py:1068
  177.1 26.2 %collective-permute-start.14 = (bf16[72,768]{1,0:T(8,128)(2,1)S(1)}, bf16[72,768]{1,0:T(8,128)(2,1)S(1)}, u32[]{:S(2)}, u32[]{:S(2)}) collective-permute-start(bf16[72,768]{1,0:T(8,128)(2,1)S(1)} %add.69.refs_0_), channel_id=1, source_target_pairs={{0,2},{1,3},{2,0},{3,1},{4,6},{5,7},{6,4},{7,5},{8,10},{9,11},{10,... | collective-permute-start | bytes 331784 | tf_op jit(solution)/shard_map/ppermute | solution.py:1068
  177.1 26.2 %collective-permute-start.13 = (bf16[72,768]{1,0:T(8,128)(2,1)S(1)}, bf16[72,768]{1,0:T(8,128)(2,1)S(1)}, u32[]{:S(2)}, u32[]{:S(2)}) collective-permute-start(bf16[72,768]{1,0:T(8,128)(2,1)S(1)} %add.69.refs_0_), channel_id=1, source_target_pairs={{0,1},{1,0},{2,3},{3,2},{4,5},{5,4},{6,7},{7,6},{8,9},{9,8},{10,11... | collective-permute-start | bytes 331784 | tf_op jit(solution)/shard_map/ppermute | solution.py:1068

commit v3 on v2

--- a/solution.py
+++ b/solution.py
@@ -640,16 +640,20 @@
 
         def begin():
             r.copy("h", 0).start()
-            for item in (qkv, out, mats, vecs):
+            qkv.start()
+            zero(r.stats)
+
+        def go_on():
+            for item in (out, mats, vecs):
                 item.start()
             for slot in range(1, slots):
                 r.copy("h", slot).start()
-            zero(r.stats)
 
         r.at_first(begin)
         live_column(r.valid, r.level, r.live)
         r.wait("h")
         qkv_phase(r.h, r.qkv.at[0], r.packed, lambda at: at % 3 or r.at_first(lambda: qkv.wait(at // 3)))
+        r.at_first(go_on)
         r.start("packed")
 
         def pair_copy_of(slot, pair, length):
@@ -662,11 +666,12 @@
         r.start("context", "linv")
         r.at_first(lambda: [item.wait() for item in (out, mats, vecs)] and None)
         project(r.context, r.out.at[0], r.attended)
+        r.start("attended")
         saved = (r.act1, r.slope1, r.std1, r.scale1)
         adapter_norm(
             r.h, r.attended, r.live, adapter_of(r.mats, r.vecs, 0), saved, r.middle, r.stats
         )
-        r.start("middle", *norm_saved(rows, width))
+        r.start("middle", *(n for n in norm_saved(rows, width) if n != "attended"))
 
         def finish():
             for slot in range(slots):
@@ -763,11 +768,13 @@
             for item in (mats0, vecs0):
                 item.start()
             base_copy(0).start()
-            for item in (win0, wout0, qkv, out1, mats1, vecs1, out0):
+            for item in (win0, wout0):
                 item.start()
             zero(r.grads, r.sums)
             for item in (mats0, vecs0, win0, wout0):
                 item.wait()
+            for item in (qkv, out1, mats1, vecs1, out0):
+                item.start()
 
         def later(act):
             pl.when(r.step > 0)(act)
@@ -938,18 +945,26 @@
                     pltpu.make_async_copy(r.stage.at[n], r.result.at[target], r.out_sems.at[n])
                 )
 
+        def start_pairs(slot, some):
+            def starts(length):
+                for pair in some:
+                    pair_copy_of(slot, pair, length).start()
+
+            by_level(r.level_of(slot), starts)
+
         def begin():
-            for slot in range(slots):
+            for name in loads:
+                r.copy(name, 0).start()
+            start_pairs(0, range(2))
+
+        def go_on():
+            start_pairs(0, range(2, pairs))
+            fill.start()
+            r.copy("dfirst", 0).start()
+            for slot in range(1, slots):
                 for name in loads:
                     r.copy(name, slot).start()
-
-                def starts(length):
-                    for pair in range(pairs):
-                        pair_copy_of(slot, pair, length).start()
-
-                by_level(r.level_of(slot), starts)
-                if slot == 0:
-                    fill.start()
+                start_pairs(slot, range(pairs))
                 r.copy("dfirst", slot).start()
             for item in ins:
                 item.start()
@@ -962,6 +977,7 @@
 
         r.at_first(begin)
         r.wait(*loads)
+        r.at_first(go_on)
         attention_backward(
             r.level, r.packed, r.context, r.held.at[r.step], r.linv, r.dcontext, r.packed,
             r.step, pair_copy_of,

time: 205 us -> 200 us (0.976)
  Pallas kernels: 161 us -> 156 us
    pallas_call x3, Pallas kernels: 158 us -> 154 us  [run(): pl.pallas_call(kernel, out_shape=self.outs, grid_spec=pltpu.PrefetchScala...]
  transfers between devices with their start and end apart: 16 -> 16, of which waited for: 7 -> 7; matrix products, arithmetic and copies ran while one was open for 1% -> 1% of each run, Pallas kernels for 23% -> 22%
where the time goes in v3:
time: 200 us
  Pallas kernels  156 us (78%)
  waiting for transfers between devices  20.3 us (10%)
  starting transfers between devices  19.8 us (10%)
  other arithmetic  2.09 us (1%)
    pallas_call x3, Pallas kernels, run(): pl.pallas_call(kernel, out_shape=self.outs, grid_spec=pltpu.PrefetchScala...  154 us
    ppermute x8, waiting for transfers between devices, exchanged(): return lax.ppermute(value, 'dp', [(at, at ^ bits) for at in range(count)])  12.7 us
    ppermute x8, starting transfers between devices, exchanged(): return lax.ppermute(value, 'dp', [(at, at ^ bits) for at in range(count)])  12.6 us
    ppermute x8, waiting for transfers between devices, swap(): return lax.ppermute(value, 'section', [(0, 1), (1, 0)])  7.61 us
    ppermute x8, starting transfers between devices, swap(): return lax.ppermute(value, 'section', [(0, 1), (1, 0)])  7.28 us
  transfers between devices with their start and end apart: 16, of which 7 were waited for; matrix products, arithmetic and copies ran while one was open for 1% of the time, Pallas kernels for 22%

profile of v3, /device:TPU:0, one launch (start us, length us, event | category | flops | bytes accessed | tf_op | source)
XLA Modules:
  0.0 200.0 jit_solution(14104049122479653478)
XLA Ops:
  0.6 0.5 collective-permute-start
  1.2 0.1 collective-permute-start.1
  1.2 1.9 pack.1
  3.1 0.4 collective-permute-start.2
  3.6 0.1 collective-permute-start.3
  3.7 5.8 %collective-permute-done.3.refs_9_.refs_20_ = f32[2,4,768]{2,1,0:T(4,128)S(1)} collective-permute-done((f32[2,4,768]{2,1,0:T(4,128)}, f32[2,4,768]{2,1,0:T(4,128)S(1)}, u32[]{:S(2)}, u32[]{:S(2)}) %collective-permute-start.3) | collective-permute-done | bytes 24608 | tf_op jit(solution)/shard_map/ppermute | solution.py:1075
  9.4 0.0 copy-start.3
  9.4 0.0 collective-permute-done.2.refs_7_.refs_18_
  9.4 0.0 copy-start.2
  9.4 0.0 collective-permute-done.1.refs_5_.refs_12_
  9.4 0.0 copy-start.1
  9.5 0.2 collective-permute-done.refs_3_.refs_10_.refs_7_
  9.6 0.4 collective-permute-start.4
  10.0 0.1 collective-permute-start.5
  10.2 0.0 copy-done.3
  10.2 0.1 copy-done.2
  10.2 0.4 copy-done.1
  10.6 20.6 %first_attn.1 = (bf16[2,512,2304]{2,1,0:T(8,128)(2,1)}, bf16[2,512,768]{2,1,0:T(8,128)(2,1)}, bf16[2,512,768]{2,1,0:T(8,128)(2,1)}, bf16[2,512,768]{2,1,0:T(8,12...) custom-call(s32[1]{0:T(128)} %bitcast.section, ...), custom_call_target="tpu_custom_call" | custom-call | flops 14495514624 | bytes 1048576 | tf_op jit(solution)/shard_map/first_attn/pallas_call | solution.py:494
  31.2 0.0 collective-permute-done.4.refs_14_
  31.2 0.0 collective-permute-done.5.refs_16_
  31.2 110.4 %middle_part.1 = (bf16[2,512,768]{2,1,0:T(8,128)(2,1)}, bf16[2,512,768]{2,1,0:T(8,128)(2,1)}, bf16[2,512,768]{2,1,0:T(8,128)(2,1)}, bf16[4,72,768]{2,1,0:T(8,128)(2,1)}, bf16[4,72,768]{2,1,0:T(8,128)(2,1)}) custom-call(s32[1]{0:T(128)} %bitcast.section, bf16[2,512,768]{2,1,0:T(8,128)(2,1)} %get-tuple-element.58.refs_0_, bf16[4,512,768]{2,1,0:T(8,128)(2,1)} %refs_1_.5, ...), custom_call_target="tpu_custom_call" | custom-call | flops 86973087744 | bytes 1048576 | tf_op jit(solution)/shard_map/middle_part/pallas_call | solution.py:494
  141.7 5.3 %collective-permute-start.6 = (bf16[4,72,768]{2,1,0:T(8,128)(2,1)}, bf16[4,72,768]{2,1,0:T(8,128)(2,1)S(1)}, u32[]{:S(2)}, u32[]{:S(2)}) collective-permute-start(bf16[4,72,768]{2,1,0:T(8,128)(2,1)} %get-tuple-element.73), channel_id=1, source_target_pairs={{0,16},{16,0},{1,17},{17,1},{2,18},{18,2},{3,19},{19,3},{4,20},{20... | collective-permute-start | bytes 1327112 | tf_op jit(solution)/shard_map/ppermute | solution.py:1075
  147.0 1.6 collective-permute-done.6
  148.6 0.4 collective-permute-start.7
  149.0 1.0 add_bitcast_fusion.2
  150.0 3.8 %collective-permute-start.10 = (bf16[72,768]{1,0:T(8,128)(2,1)S(1)}, bf16[72,768]{1,0:T(8,128)(2,1)S(1)}, u32[]{:S(2)}, u32[]{:S(2)}) collective-permute-start(bf16[72,768]{1,0:T(8,128)(2,1)S(1)} %get-tuple-element.96), channel_id=1, source_target_pairs={{0,3},{1,2},{2,1},{3,0},{4,7},{5,6},{6,5},{7,4},{8,11},{9,10},{10,... | collective-permute-start | bytes 331784 | tf_op jit(solution)/shard_map/ppermute | solution.py:1084
  153.9 0.5 collective-permute-start.8
  154.4 0.1 collective-permute-start.9
  154.5 3.2 %collective-permute-done.10 = bf16[72,768]{1,0:T(8,128)(2,1)S(1)} collective-permute-done((bf16[72,768]{1,0:T(8,128)(2,1)S(1)}, bf16[72,768]{1,0:T(8,128)(2,1)S(1)}, u32[]{:S(2)}, u32[]{:S(2)}) %collective-permute-start.10) | collective-permute-done | bytes 110624 | tf_op jit(solution)/shard_map/ppermute | solution.py:1084
  157.7 2.1 %collective-permute-done.8 = bf16[72,768]{1,0:T(8,128)(2,1)S(1)} collective-permute-done((bf16[72,768]{1,0:T(8,128)(2,1)S(1)}, bf16[72,768]{1,0:T(8,128)(2,1)S(1)}, u32[]{:S(2)}, u32[]{:S(2)}) %collective-permute-start.8) | collective-permute-done | bytes 110624 | tf_op jit(solution)/shard_map/ppermute | solution.py:1084
  159.8 0.0 collective-permute-done.9
  159.8 1.0 fusion.1
  160.8 1.7 collective-permute-start.11
  162.5 3.2 %collective-permute-done.11 = bf16[72,768]{1,0:T(8,128)(2,1)S(1)} collective-permute-done((bf16[72,768]{1,0:T(8,128)(2,1)S(1)}, bf16[72,768]{1,0:T(8,128)(2,1)S(1)}, u32[]{:S(2)}, u32[]{:S(2)}) %collective-permute-start.11) | collective-permute-done | bytes 110624 | tf_op jit(solution)/shard_map/ppermute | solution.py:1084
  165.7 2.7 %collective-permute-start.12 = (bf16[72,768]{1,0:T(8,128)(2,1)S(1)}, bf16[72,768]{1,0:T(8,128)(2,1)S(1)}, u32[]{:S(2)}, u32[]{:S(2)}) collective-permute-start(bf16[72,768]{1,0:T(8,128)(2,1)S(1)} %add.68), channel_id=1, source_target_pairs={{0,8},{1,9},{2,10},{3,11},{4,12},{5,13},{6,14},{7,15},{8,0},{9,1},... | collective-permute-start | bytes 331784 | tf_op jit(solution)/shard_map/ppermute | solution.py:1084
  168.3 4.2 %collective-permute-done.12 = bf16[72,768]{1,0:T(8,128)(2,1)S(1)} collective-permute-done((bf16[72,768]{1,0:T(8,128)(2,1)S(1)}, bf16[72,768]{1,0:T(8,128)(2,1)S(1)}, u32[]{:S(2)}, u32[]{:S(2)}) %collective-permute-start.12) | collective-permute-done | bytes 110624 | tf_op jit(solution)/shard_map/ppermute | solution.py:1084
  172.6 0.0 collective-permute-done.7.refs_9_
  172.6 0.0 copy-start
  172.6 3.1 %collective-permute-start.15 = (bf16[72,768]{1,0:T(8,128)(2,1)S(1)}, bf16[72,768]{1,0:T(8,128)(2,1)S(1)}, u32[]{:S(2)}, u32[]{:S(2)}) collective-permute-start(bf16[72,768]{1,0:T(8,128)(2,1)S(1)} %add.69.refs_0_), channel_id=1, source_target_pairs={{0,3},{1,2},{2,1},{3,0},{4,7},{5,6},{6,5},{7,4},{8,11},{9,10},{10,... | collective-permute-start | bytes 331784 | tf_op jit(solution)/shard_map/ppermute | solution.py:1084
  175.7 0.0 collective-permute-start.14
  175.7 0.7 collective-permute-start.13
  176.4 0.0 copy-done
  176.4 22.5 %attn_back.1 = (bf16[2,512,768]{2,1,0:T(8,128)(2,1)}, bf16[4,512,768]{2,1,0:T(8,128)(2,1)}) custom-call(s32[1]{0:T(128)} %bitcast.section, bf16[2,512,2304]{2,1,0:T(8,128)(2,1)} %get-tuple-element.57.refs_0_, bf16[2,512,768]{2,1,0:T(8,128)(2,1)} %get-tuple-element.67.refs_1_, bf16[2,512,768]{2,1,0:T(8,128)(2,1)} %get-tuple-element.68.refs_2_, ...), custom_call_target="tpu_custom_call" | custom-call | flops 14495514624 | bytes 1048576 | tf_op jit(solution)/shard_map/attn_back/pallas_call | solution.py:494
  198.9 0.0 collective-permute-done.15.refs_3_
  198.9 0.0 collective-permute-done.14.refs_2_
  198.9 0.0 collective-permute-done.13.refs_1_
  198.9 1.0 unpack.1
  (2 shorter events, 0.1 us)
Async XLA Ops:
  0.6 9.0 %collective-permute-start = (bf16[1,768,2304]{2,1,0:T(8,128)(2,1)}, bf16[1,768,2304]{2,1,0:T(8,128)(2,1)}, u32[]{:S(2)}, u32[]{:S(2)}) collective-permute-start(bf16[1,768,2304]{2,1,0:T(8,128)(2,1)} %refs_6_.3), channel_id=1, source_target_pairs={{0,16},{16,0},{1,17},{17,1},{2,18},{18,2},{3,19},{19,3},{4,20},{20... | collective-permute-start | bytes 10616840 | tf_op jit(solution)/shard_map/ppermute | solution.py:1075
  1.2 8.3 %collective-permute-start.1 = (bf16[1,768,768]{2,1,0:T(8,128)(2,1)}, bf16[1,768,768]{2,1,0:T(8,128)(2,1)S(1)}, u32[]{:S(2)}, u32[]{:S(2)}) collective-permute-start(bf16[1,768,768]{2,1,0:T(8,128)(2,1)} %refs_11_.3), channel_id=1, source_target_pairs={{0,16},{16,0},{1,17},{17,1},{2,18},{18,2},{3,19},{19,3},{4,20},{20... | collective-permute-start | bytes 3538952 | tf_op jit(solution)/shard_map/ppermute | solution.py:1075
  3.1 6.3 %collective-permute-start.2 = (bf16[4,64,768]{2,1,0:T(8,128)(2,1)}, bf16[4,64,768]{2,1,0:T(8,128)(2,1)S(1)}, u32[]{:S(2)}, u32[]{:S(2)}) collective-permute-start(bf16[4,64,768]{2,1,0:T(8,128)(2,1)} %get-tuple-element.55.refs_6_.refs_17_), channel_id=1, source_target_pairs={{0,16},{16,0},{1,17},{17,1},{2,18},{18,2},{3,19},{19,3},{4,20},{20... | collective-permute-start | bytes 1179656 | tf_op jit(solution)/shard_map/ppermute | solution.py:1075
  3.6 5.9 %collective-permute-start.3 = (f32[2,4,768]{2,1,0:T(4,128)}, f32[2,4,768]{2,1,0:T(4,128)S(1)}, u32[]{:S(2)}, u32[]{:S(2)}) collective-permute-start(f32[2,4,768]{2,1,0:T(4,128)} %get-tuple-element.56.refs_8_.refs_19_), channel_id=1, source_target_pairs={{0,16},{16,0},{1,17},{17,1},{2,18},{18,2},{3,19},{19,3},{4,20},{20... | collective-permute-start | bytes 73736 | tf_op jit(solution)/shard_map/ppermute | solution.py:1075
  9.4 0.7 copy-start.3
  9.4 0.8 copy-start.2
  9.4 1.2 copy-start.1
  9.6 21.6 %collective-permute-start.4 = (bf16[1,768,3072]{2,1,0:T(8,128)(2,1)}, bf16[1,768,3072]{2,1,0:T(8,128)(2,1)}, u32[]{:S(2)}, u32[]{:S(2)}) collective-permute-start(bf16[1,768,3072]{2,1,0:T(8,128)(2,1)} %refs_13_.1), channel_id=1, source_target_pairs={{0,16},{16,0},{1,17},{17,1},{2,18},{18,2},{3,19},{19,3},{4,20},{20... | collective-permute-start | bytes 14155784 | tf_op jit(solution)/shard_map/ppermute | solution.py:1075
  10.0 21.2 %collective-permute-start.5 = (bf16[1,3072,768]{2,1,0:T(8,128)(2,1)}, bf16[1,3072,768]{2,1,0:T(8,128)(2,1)}, u32[]{:S(2)}, u32[]{:S(2)}) collective-permute-start(bf16[1,3072,768]{2,1,0:T(8,128)(2,1)} %refs_15_.1), channel_id=1, source_target_pairs={{0,16},{16,0},{1,17},{17,1},{2,18},{18,2},{3,19},{19,3},{4,20},{20... | collective-permute-start | bytes 14155784 | tf_op jit(solution)/shard_map/ppermute | solution.py:1075
  141.7 6.9 %collective-permute-start.6 = (bf16[4,72,768]{2,1,0:T(8,128)(2,1)}, bf16[4,72,768]{2,1,0:T(8,128)(2,1)S(1)}, u32[]{:S(2)}, u32[]{:S(2)}) collective-permute-start(bf16[4,72,768]{2,1,0:T(8,128)(2,1)} %get-tuple-element.73), channel_id=1, source_target_pairs={{0,16},{16,0},{1,17},{17,1},{2,18},{18,2},{3,19},{19,3},{4,20},{20... | collective-permute-start | bytes 1327112 | tf_op jit(solution)/shard_map/ppermute | solution.py:1075
  148.6 24.0 %collective-permute-start.7 = (bf16[2,512,768]{2,1,0:T(8,128)(2,1)}, bf16[2,512,768]{2,1,0:T(8,128)(2,1)S(1)}, u32[]{:S(2)}, u32[]{:S(2)}) collective-permute-start(bf16[2,512,768]{2,1,0:T(8,128)(2,1)} %get-tuple-element.74.refs_8_), channel_id=1, source_target_pairs={{0,16},{16,0},{1,17},{17,1},{2,18},{18,2},{3,19},{19,3},{4,20},{20... | collective-permute-start | bytes 4718600 | tf_op jit(solution)/shard_map/ppermute | solution.py:1075
  150.0 7.7 %collective-permute-start.10 = (bf16[72,768]{1,0:T(8,128)(2,1)S(1)}, bf16[72,768]{1,0:T(8,128)(2,1)S(1)}, u32[]{:S(2)}, u32[]{:S(2)}) collective-permute-start(bf16[72,768]{1,0:T(8,128)(2,1)S(1)} %get-tuple-element.96), channel_id=1, source_target_pairs={{0,3},{1,2},{2,1},{3,0},{4,7},{5,6},{6,5},{7,4},{8,11},{9,10},{10,... | collective-permute-start | bytes 331784 | tf_op jit(solution)/shard_map/ppermute | solution.py:1084
  153.9 6.0 %collective-permute-start.8 = (bf16[72,768]{1,0:T(8,128)(2,1)S(1)}, bf16[72,768]{1,0:T(8,128)(2,1)S(1)}, u32[]{:S(2)}, u32[]{:S(2)}) collective-permute-start(bf16[72,768]{1,0:T(8,128)(2,1)S(1)} %get-tuple-element.95), channel_id=1, source_target_pairs={{0,1},{1,0},{2,3},{3,2},{4,5},{5,4},{6,7},{7,6},{8,9},{9,8},{10,11... | collective-permute-start | bytes 331784 | tf_op jit(solution)/shard_map/ppermute | solution.py:1084
  154.4 5.4 %collective-permute-start.9 = (bf16[72,768]{1,0:T(8,128)(2,1)S(1)}, bf16[72,768]{1,0:T(8,128)(2,1)S(1)}, u32[]{:S(2)}, u32[]{:S(2)}) collective-permute-start(bf16[72,768]{1,0:T(8,128)(2,1)S(1)} %get-tuple-element.97), channel_id=1, source_target_pairs={{0,2},{1,3},{2,0},{3,1},{4,6},{5,7},{6,4},{7,5},{8,10},{9,11},{10,... | collective-permute-start | bytes 331784 | tf_op jit(solution)/shard_map/ppermute | solution.py:1084
  160.8 4.8 %collective-permute-start.11 = (bf16[72,768]{1,0:T(8,128)(2,1)S(1)}, bf16[72,768]{1,0:T(8,128)(2,1)S(1)}, u32[]{:S(2)}, u32[]{:S(2)}) collective-permute-start(bf16[72,768]{1,0:T(8,128)(2,1)S(1)} %fusion.1), channel_id=1, source_target_pairs={{0,4},{1,5},{2,6},{3,7},{4,0},{5,1},{6,2},{7,3},{8,12},{9,13},{10,... | collective-permute-start | bytes 331784 | tf_op jit(solution)/shard_map/ppermute | solution.py:1084
  165.7 6.9 %collective-permute-start.12 = (bf16[72,768]{1,0:T(8,128)(2,1)S(1)}, bf16[72,768]{1,0:T(8,128)(2,1)S(1)}, u32[]{:S(2)}, u32[]{:S(2)}) collective-permute-start(bf16[72,768]{1,0:T(8,128)(2,1)S(1)} %add.68), channel_id=1, source_target_pairs={{0,8},{1,9},{2,10},{3,11},{4,12},{5,13},{6,14},{7,15},{8,0},{9,1},... | collective-permute-start | bytes 331784 | tf_op jit(solution)/shard_map/ppermute | solution.py:1084
  172.6 3.8 %copy-start = (bf16[2,512,768]{2,1,0:T(8,128)(2,1)}, bf16[2,512,768]{2,1,0:T(8,128)(2,1)S(1)}, u32[]{:S(2)}) copy-start(bf16[2,512,768]{2,1,0:T(8,128)(2,1)S(1)} %collective-permute-done.7.refs_9_) | copy-start | bytes 4718596
  172.6 26.3 %collective-permute-start.15 = (bf16[72,768]{1,0:T(8,128)(2,1)S(1)}, bf16[72,768]{1,0:T(8,128)(2,1)S(1)}, u32[]{:S(2)}, u32[]{:S(2)}) collective-permute-start(bf16[72,768]{1,0:T(8,128)(2,1)S(1)} %add.69.refs_0_), channel_id=1, source_target_pairs={{0,3},{1,2},{2,1},{3,0},{4,7},{5,6},{6,5},{7,4},{8,11},{9,10},{10,... | collective-permute-start | bytes 331784 | tf_op jit(solution)/shard_map/ppermute | solution.py:1084
  175.7 23.2 %collective-permute-start.14 = (bf16[72,768]{1,0:T(8,128)(2,1)S(1)}, bf16[72,768]{1,0:T(8,128)(2,1)S(1)}, u32[]{:S(2)}, u32[]{:S(2)}) collective-permute-start(bf16[72,768]{1,0:T(8,128)(2,1)S(1)} %add.69.refs_0_), channel_id=1, source_target_pairs={{0,2},{1,3},{2,0},{3,1},{4,6},{5,7},{6,4},{7,5},{8,10},{9,11},{10,... | collective-permute-start | bytes 331784 | tf_op jit(solution)/shard_map/ppermute | solution.py:1084
  175.7 23.2 %collective-permute-start.13 = (bf16[72,768]{1,0:T(8,128)(2,1)S(1)}, bf16[72,768]{1,0:T(8,128)(2,1)S(1)}, u32[]{:S(2)}, u32[]{:S(2)}) collective-permute-start(bf16[72,768]{1,0:T(8,128)(2,1)S(1)} %add.69.refs_0_), channel_id=1, source_target_pairs={{0,1},{1,0},{2,3},{3,2},{4,5},{5,4},{6,7},{7,6},{8,9},{9,8},{10,11... | collective-permute-start | bytes 331784 | tf_op jit(solution)/shard_map/ppermute | solution.py:1084

commit v4 on v3

--- a/solution.py
+++ b/solution.py
@@ -180,7 +180,7 @@
     by_level(level, run)
 
 
-def attention_backward(level, packed, context, portions, linv, dcontext, dpacked, slot=0, copy=None):
+def attention_backward(level, packed, context, portions, linv, dcontext, dpacked, slot=0, copy=None, short_pairs=1):
     rows, width = context.shape
     query = 256
 
@@ -220,7 +220,7 @@
                 dpacked[whole, span_of(at, 128, width)] = dk.astype(BF)
                 dpacked[whole, span_of(at, 128, 2 * width)] = dv.astype(BF)
 
-        steps(width // 128, pair, PAIRS_BACKWARD)
+        steps(width // 128, pair, short_pairs if length == 256 else PAIRS_BACKWARD)
 
     by_level(level, run)
 
@@ -875,7 +875,8 @@
                 @pl.when(at == 1)
                 def _():
                     attention_backward(
-                        r.level, r.packed, r.context, r.held, r.linv, r.dcontext0, r.packed
+                        r.level, r.packed, r.context, r.held, r.linv, r.dcontext0, r.packed,
+                        short_pairs=2,
                     )
                     input_backward(r.packed, r.qkv.at[0], r.dsum, r.up)
 

time: 200 us -> 200 us (level)
  no operation moved by 1% of the time
where the time goes in v4:
time: 200 us
  Pallas kernels  157 us (78%)
  waiting for transfers between devices  20.3 us (10%)
  starting transfers between devices  19.8 us (10%)
  other arithmetic  2.09 us (1%)
    pallas_call x3, Pallas kernels, run(): pl.pallas_call(kernel, out_shape=self.outs, grid_spec=pltpu.PrefetchScala...  154 us
    ppermute x8, waiting for transfers between devices, exchanged(): return lax.ppermute(value, 'dp', [(at, at ^ bits) for at in range(count)])  12.7 us
    ppermute x8, starting transfers between devices, exchanged(): return lax.ppermute(value, 'dp', [(at, at ^ bits) for at in range(count)])  12.6 us
    ppermute x8, waiting for transfers between devices, swap(): return lax.ppermute(value, 'section', [(0, 1), (1, 0)])  7.61 us
    ppermute x8, starting transfers between devices, swap(): return lax.ppermute(value, 'section', [(0, 1), (1, 0)])  7.22 us
  transfers between devices with their start and end apart: 16, of which 7 were waited for; matrix products, arithmetic and copies ran while one was open for 1% of the time, Pallas kernels for 22%

profile of v4, /device:TPU:0, one launch (start us, length us, event | category | flops | bytes accessed | tf_op | source)
XLA Modules:
  0.0 200.1 jit_solution(10763644340372594472)
XLA Ops:
  0.6 0.5 collective-permute-start
  1.2 0.1 collective-permute-start.1
  1.2 1.9 pack.1
  3.1 0.4 collective-permute-start.2
  3.6 0.1 collective-permute-start.3
  3.7 5.8 %collective-permute-done.3.refs_9_.refs_20_ = f32[2,4,768]{2,1,0:T(4,128)S(1)} collective-permute-done((f32[2,4,768]{2,1,0:T(4,128)}, f32[2,4,768]{2,1,0:T(4,128)S(1)}, u32[]{:S(2)}, u32[]{:S(2)}) %collective-permute-start.3) | collective-permute-done | bytes 24608 | tf_op jit(solution)/shard_map/ppermute | solution.py:1076
  9.4 0.0 copy-start.3
  9.4 0.0 collective-permute-done.2.refs_7_.refs_18_
  9.4 0.0 copy-start.2
  9.4 0.0 collective-permute-done.1.refs_5_.refs_12_
  9.4 0.0 copy-start.1
  9.5 0.2 collective-permute-done.refs_3_.refs_10_.refs_7_
  9.6 0.4 collective-permute-start.4
  10.0 0.1 collective-permute-start.5
  10.2 0.0 copy-done.3
  10.2 0.1 copy-done.2
  10.2 0.4 copy-done.1
  10.6 20.6 %first_attn.1 = (bf16[2,512,2304]{2,1,0:T(8,128)(2,1)}, bf16[2,512,768]{2,1,0:T(8,128)(2,1)}, bf16[2,512,768]{2,1,0:T(8,128)(2,1)}, bf16[2,512,768]{2,1,0:T(8,12...) custom-call(s32[1]{0:T(128)} %bitcast.section, ...), custom_call_target="tpu_custom_call" | custom-call | flops 14495514624 | bytes 1048576 | tf_op jit(solution)/shard_map/first_attn/pallas_call | solution.py:494
  31.2 0.0 collective-permute-done.4.refs_14_
  31.2 0.0 collective-permute-done.5.refs_16_
  31.2 110.5 %middle_part.1 = (bf16[2,512,768]{2,1,0:T(8,128)(2,1)}, bf16[2,512,768]{2,1,0:T(8,128)(2,1)}, bf16[2,512,768]{2,1,0:T(8,128)(2,1)}, bf16[4,72,768]{2,1,0:T(8,128)(2,1)}, bf16[4,72,768]{2,1,0:T(8,128)(2,1)}) custom-call(s32[1]{0:T(128)} %bitcast.section, bf16[2,512,768]{2,1,0:T(8,128)(2,1)} %get-tuple-element.58.refs_0_, bf16[4,512,768]{2,1,0:T(8,128)(2,1)} %refs_1_.5, ...), custom_call_target="tpu_custom_call" | custom-call | flops 86973087744 | bytes 1048576 | tf_op jit(solution)/shard_map/middle_part/pallas_call | solution.py:494
  141.8 5.2 %collective-permute-start.6 = (bf16[4,72,768]{2,1,0:T(8,128)(2,1)}, bf16[4,72,768]{2,1,0:T(8,128)(2,1)S(1)}, u32[]{:S(2)}, u32[]{:S(2)}) collective-permute-start(bf16[4,72,768]{2,1,0:T(8,128)(2,1)} %get-tuple-element.73), channel_id=1, source_target_pairs={{0,16},{16,0},{1,17},{17,1},{2,18},{18,2},{3,19},{19,3},{4,20},{20... | collective-permute-start | bytes 1327112 | tf_op jit(solution)/shard_map/ppermute | solution.py:1076
  147.0 1.6 collective-permute-done.6
  148.6 0.4 collective-permute-start.7
  149.0 1.0 add_bitcast_fusion.2
  150.0 3.8 %collective-permute-start.10 = (bf16[72,768]{1,0:T(8,128)(2,1)S(1)}, bf16[72,768]{1,0:T(8,128)(2,1)S(1)}, u32[]{:S(2)}, u32[]{:S(2)}) collective-permute-start(bf16[72,768]{1,0:T(8,128)(2,1)S(1)} %get-tuple-element.96), channel_id=1, source_target_pairs={{0,3},{1,2},{2,1},{3,0},{4,7},{5,6},{6,5},{7,4},{8,11},{9,10},{10,... | collective-permute-start | bytes 331784 | tf_op jit(solution)/shard_map/ppermute | solution.py:1085
  153.9 0.5 collective-permute-start.8
  154.4 0.1 collective-permute-start.9
  154.5 3.2 %collective-permute-done.10 = bf16[72,768]{1,0:T(8,128)(2,1)S(1)} collective-permute-done((bf16[72,768]{1,0:T(8,128)(2,1)S(1)}, bf16[72,768]{1,0:T(8,128)(2,1)S(1)}, u32[]{:S(2)}, u32[]{:S(2)}) %collective-permute-start.10) | collective-permute-done | bytes 110624 | tf_op jit(solution)/shard_map/ppermute | solution.py:1085
  157.7 2.1 %collective-permute-done.8 = bf16[72,768]{1,0:T(8,128)(2,1)S(1)} collective-permute-done((bf16[72,768]{1,0:T(8,128)(2,1)S(1)}, bf16[72,768]{1,0:T(8,128)(2,1)S(1)}, u32[]{:S(2)}, u32[]{:S(2)}) %collective-permute-start.8) | collective-permute-done | bytes 110624 | tf_op jit(solution)/shard_map/ppermute | solution.py:1085
  159.8 0.0 collective-permute-done.9
  159.8 1.0 fusion.1
  160.8 1.7 collective-permute-start.11
  162.5 3.2 %collective-permute-done.11 = bf16[72,768]{1,0:T(8,128)(2,1)S(1)} collective-permute-done((bf16[72,768]{1,0:T(8,128)(2,1)S(1)}, bf16[72,768]{1,0:T(8,128)(2,1)S(1)}, u32[]{:S(2)}, u32[]{:S(2)}) %collective-permute-start.11) | collective-permute-done | bytes 110624 | tf_op jit(solution)/shard_map/ppermute | solution.py:1085
  165.7 2.7 %collective-permute-start.12 = (bf16[72,768]{1,0:T(8,128)(2,1)S(1)}, bf16[72,768]{1,0:T(8,128)(2,1)S(1)}, u32[]{:S(2)}, u32[]{:S(2)}) collective-permute-start(bf16[72,768]{1,0:T(8,128)(2,1)S(1)} %add.68), channel_id=1, source_target_pairs={{0,8},{1,9},{2,10},{3,11},{4,12},{5,13},{6,14},{7,15},{8,0},{9,1},... | collective-permute-start | bytes 331784 | tf_op jit(solution)/shard_map/ppermute | solution.py:1085
  168.3 4.2 %collective-permute-done.12 = bf16[72,768]{1,0:T(8,128)(2,1)S(1)} collective-permute-done((bf16[72,768]{1,0:T(8,128)(2,1)S(1)}, bf16[72,768]{1,0:T(8,128)(2,1)S(1)}, u32[]{:S(2)}, u32[]{:S(2)}) %collective-permute-start.12) | collective-permute-done | bytes 110624 | tf_op jit(solution)/shard_map/ppermute | solution.py:1085
  172.6 0.0 collective-permute-done.7.refs_9_
  172.6 0.0 copy-start
  172.6 3.1 %collective-permute-start.15 = (bf16[72,768]{1,0:T(8,128)(2,1)S(1)}, bf16[72,768]{1,0:T(8,128)(2,1)S(1)}, u32[]{:S(2)}, u32[]{:S(2)}) collective-permute-start(bf16[72,768]{1,0:T(8,128)(2,1)S(1)} %add.69.refs_0_), channel_id=1, source_target_pairs={{0,3},{1,2},{2,1},{3,0},{4,7},{5,6},{6,5},{7,4},{8,11},{9,10},{10,... | collective-permute-start | bytes 331784 | tf_op jit(solution)/shard_map/ppermute | solution.py:1085
  175.7 0.0 collective-permute-start.14
  175.7 0.7 collective-permute-start.13
  176.4 0.0 copy-done
  176.4 22.5 %attn_back.1 = (bf16[2,512,768]{2,1,0:T(8,128)(2,1)}, bf16[4,512,768]{2,1,0:T(8,128)(2,1)}) custom-call(s32[1]{0:T(128)} %bitcast.section, bf16[2,512,2304]{2,1,0:T(8,128)(2,1)} %get-tuple-element.57.refs_0_, bf16[2,512,768]{2,1,0:T(8,128)(2,1)} %get-tuple-element.67.refs_1_, bf16[2,512,768]{2,1,0:T(8,128)(2,1)} %get-tuple-element.68.refs_2_, ...), custom_call_target="tpu_custom_call" | custom-call | flops 14495514624 | bytes 1048576 | tf_op jit(solution)/shard_map/attn_back/pallas_call | solution.py:494
  198.9 0.0 collective-permute-done.15.refs_3_
  198.9 0.0 collective-permute-done.14.refs_2_
  198.9 0.0 collective-permute-done.13.refs_1_
  198.9 1.0 unpack.1
  (2 shorter events, 0.1 us)
Async XLA Ops:
  0.6 9.0 %collective-permute-start = (bf16[1,768,2304]{2,1,0:T(8,128)(2,1)}, bf16[1,768,2304]{2,1,0:T(8,128)(2,1)}, u32[]{:S(2)}, u32[]{:S(2)}) collective-permute-start(bf16[1,768,2304]{2,1,0:T(8,128)(2,1)} %refs_6_.3), channel_id=1, source_target_pairs={{0,16},{16,0},{1,17},{17,1},{2,18},{18,2},{3,19},{19,3},{4,20},{20... | collective-permute-start | bytes 10616840 | tf_op jit(solution)/shard_map/ppermute | solution.py:1076
  1.2 8.3 %collective-permute-start.1 = (bf16[1,768,768]{2,1,0:T(8,128)(2,1)}, bf16[1,768,768]{2,1,0:T(8,128)(2,1)S(1)}, u32[]{:S(2)}, u32[]{:S(2)}) collective-permute-start(bf16[1,768,768]{2,1,0:T(8,128)(2,1)} %refs_11_.3), channel_id=1, source_target_pairs={{0,16},{16,0},{1,17},{17,1},{2,18},{18,2},{3,19},{19,3},{4,20},{20... | collective-permute-start | bytes 3538952 | tf_op jit(solution)/shard_map/ppermute | solution.py:1076
  3.1 6.3 %collective-permute-start.2 = (bf16[4,64,768]{2,1,0:T(8,128)(2,1)}, bf16[4,64,768]{2,1,0:T(8,128)(2,1)S(1)}, u32[]{:S(2)}, u32[]{:S(2)}) collective-permute-start(bf16[4,64,768]{2,1,0:T(8,128)(2,1)} %get-tuple-element.55.refs_6_.refs_17_), channel_id=1, source_target_pairs={{0,16},{16,0},{1,17},{17,1},{2,18},{18,2},{3,19},{19,3},{4,20},{20... | collective-permute-start | bytes 1179656 | tf_op jit(solution)/shard_map/ppermute | solution.py:1076
  3.6 5.9 %collective-permute-start.3 = (f32[2,4,768]{2,1,0:T(4,128)}, f32[2,4,768]{2,1,0:T(4,128)S(1)}, u32[]{:S(2)}, u32[]{:S(2)}) collective-permute-start(f32[2,4,768]{2,1,0:T(4,128)} %get-tuple-element.56.refs_8_.refs_19_), channel_id=1, source_target_pairs={{0,16},{16,0},{1,17},{17,1},{2,18},{18,2},{3,19},{19,3},{4,20},{20... | collective-permute-start | bytes 73736 | tf_op jit(solution)/shard_map/ppermute | solution.py:1076
  9.4 0.7 copy-start.3
  9.4 0.8 copy-start.2
  9.4 1.2 copy-start.1
  9.6 21.6 %collective-permute-start.4 = (bf16[1,768,3072]{2,1,0:T(8,128)(2,1)}, bf16[1,768,3072]{2,1,0:T(8,128)(2,1)}, u32[]{:S(2)}, u32[]{:S(2)}) collective-permute-start(bf16[1,768,3072]{2,1,0:T(8,128)(2,1)} %refs_13_.1), channel_id=1, source_target_pairs={{0,16},{16,0},{1,17},{17,1},{2,18},{18,2},{3,19},{19,3},{4,20},{20... | collective-permute-start | bytes 14155784 | tf_op jit(solution)/shard_map/ppermute | solution.py:1076
  10.0 21.2 %collective-permute-start.5 = (bf16[1,3072,768]{2,1,0:T(8,128)(2,1)}, bf16[1,3072,768]{2,1,0:T(8,128)(2,1)}, u32[]{:S(2)}, u32[]{:S(2)}) collective-permute-start(bf16[1,3072,768]{2,1,0:T(8,128)(2,1)} %refs_15_.1), channel_id=1, source_target_pairs={{0,16},{16,0},{1,17},{17,1},{2,18},{18,2},{3,19},{19,3},{4,20},{20... | collective-permute-start | bytes 14155784 | tf_op jit(solution)/shard_map/ppermute | solution.py:1076
  141.8 6.9 %collective-permute-start.6 = (bf16[4,72,768]{2,1,0:T(8,128)(2,1)}, bf16[4,72,768]{2,1,0:T(8,128)(2,1)S(1)}, u32[]{:S(2)}, u32[]{:S(2)}) collective-permute-start(bf16[4,72,768]{2,1,0:T(8,128)(2,1)} %get-tuple-element.73), channel_id=1, source_target_pairs={{0,16},{16,0},{1,17},{17,1},{2,18},{18,2},{3,19},{19,3},{4,20},{20... | collective-permute-start | bytes 1327112 | tf_op jit(solution)/shard_map/ppermute | solution.py:1076
  148.6 24.0 %collective-permute-start.7 = (bf16[2,512,768]{2,1,0:T(8,128)(2,1)}, bf16[2,512,768]{2,1,0:T(8,128)(2,1)S(1)}, u32[]{:S(2)}, u32[]{:S(2)}) collective-permute-start(bf16[2,512,768]{2,1,0:T(8,128)(2,1)} %get-tuple-element.74.refs_8_), channel_id=1, source_target_pairs={{0,16},{16,0},{1,17},{17,1},{2,18},{18,2},{3,19},{19,3},{4,20},{20... | collective-permute-start | bytes 4718600 | tf_op jit(solution)/shard_map/ppermute | solution.py:1076
  150.0 7.7 %collective-permute-start.10 = (bf16[72,768]{1,0:T(8,128)(2,1)S(1)}, bf16[72,768]{1,0:T(8,128)(2,1)S(1)}, u32[]{:S(2)}, u32[]{:S(2)}) collective-permute-start(bf16[72,768]{1,0:T(8,128)(2,1)S(1)} %get-tuple-element.96), channel_id=1, source_target_pairs={{0,3},{1,2},{2,1},{3,0},{4,7},{5,6},{6,5},{7,4},{8,11},{9,10},{10,... | collective-permute-start | bytes 331784 | tf_op jit(solution)/shard_map/ppermute | solution.py:1085
  153.9 6.0 %collective-permute-start.8 = (bf16[72,768]{1,0:T(8,128)(2,1)S(1)}, bf16[72,768]{1,0:T(8,128)(2,1)S(1)}, u32[]{:S(2)}, u32[]{:S(2)}) collective-permute-start(bf16[72,768]{1,0:T(8,128)(2,1)S(1)} %get-tuple-element.95), channel_id=1, source_target_pairs={{0,1},{1,0},{2,3},{3,2},{4,5},{5,4},{6,7},{7,6},{8,9},{9,8},{10,11... | collective-permute-start | bytes 331784 | tf_op jit(solution)/shard_map/ppermute | solution.py:1085
  154.4 5.4 %collective-permute-start.9 = (bf16[72,768]{1,0:T(8,128)(2,1)S(1)}, bf16[72,768]{1,0:T(8,128)(2,1)S(1)}, u32[]{:S(2)}, u32[]{:S(2)}) collective-permute-start(bf16[72,768]{1,0:T(8,128)(2,1)S(1)} %get-tuple-element.97), channel_id=1, source_target_pairs={{0,2},{1,3},{2,0},{3,1},{4,6},{5,7},{6,4},{7,5},{8,10},{9,11},{10,... | collective-permute-start | bytes 331784 | tf_op jit(solution)/shard_map/ppermute | solution.py:1085
  160.8 4.8 %collective-permute-start.11 = (bf16[72,768]{1,0:T(8,128)(2,1)S(1)}, bf16[72,768]{1,0:T(8,128)(2,1)S(1)}, u32[]{:S(2)}, u32[]{:S(2)}) collective-permute-start(bf16[72,768]{1,0:T(8,128)(2,1)S(1)} %fusion.1), channel_id=1, source_target_pairs={{0,4},{1,5},{2,6},{3,7},{4,0},{5,1},{6,2},{7,3},{8,12},{9,13},{10,... | collective-permute-start | bytes 331784 | tf_op jit(solution)/shard_map/ppermute | solution.py:1085
  165.7 6.9 %collective-permute-start.12 = (bf16[72,768]{1,0:T(8,128)(2,1)S(1)}, bf16[72,768]{1,0:T(8,128)(2,1)S(1)}, u32[]{:S(2)}, u32[]{:S(2)}) collective-permute-start(bf16[72,768]{1,0:T(8,128)(2,1)S(1)} %add.68), channel_id=1, source_target_pairs={{0,8},{1,9},{2,10},{3,11},{4,12},{5,13},{6,14},{7,15},{8,0},{9,1},... | collective-permute-start | bytes 331784 | tf_op jit(solution)/shard_map/ppermute | solution.py:1085
  172.6 3.8 %copy-start = (bf16[2,512,768]{2,1,0:T(8,128)(2,1)}, bf16[2,512,768]{2,1,0:T(8,128)(2,1)S(1)}, u32[]{:S(2)}) copy-start(bf16[2,512,768]{2,1,0:T(8,128)(2,1)S(1)} %collective-permute-done.7.refs_9_) | copy-start | bytes 4718596
  172.6 26.3 %collective-permute-start.15 = (bf16[72,768]{1,0:T(8,128)(2,1)S(1)}, bf16[72,768]{1,0:T(8,128)(2,1)S(1)}, u32[]{:S(2)}, u32[]{:S(2)}) collective-permute-start(bf16[72,768]{1,0:T(8,128)(2,1)S(1)} %add.69.refs_0_), channel_id=1, source_target_pairs={{0,3},{1,2},{2,1},{3,0},{4,7},{5,6},{6,5},{7,4},{8,11},{9,10},{10,... | collective-permute-start | bytes 331784 | tf_op jit(solution)/shard_map/ppermute | solution.py:1085
  175.7 23.2 %collective-permute-start.14 = (bf16[72,768]{1,0:T(8,128)(2,1)S(1)}, bf16[72,768]{1,0:T(8,128)(2,1)S(1)}, u32[]{:S(2)}, u32[]{:S(2)}) collective-permute-start(bf16[72,768]{1,0:T(8,128)(2,1)S(1)} %add.69.refs_0_), channel_id=1, source_target_pairs={{0,2},{1,3},{2,0},{3,1},{4,6},{5,7},{6,4},{7,5},{8,10},{9,11},{10,... | collective-permute-start | bytes 331784 | tf_op jit(solution)/shard_map/ppermute | solution.py:1085
  175.7 23.2 %collective-permute-start.13 = (bf16[72,768]{1,0:T(8,128)(2,1)S(1)}, bf16[72,768]{1,0:T(8,128)(2,1)S(1)}, u32[]{:S(2)}, u32[]{:S(2)}) collective-permute-start(bf16[72,768]{1,0:T(8,128)(2,1)S(1)} %add.69.refs_0_), channel_id=1, source_target_pairs={{0,1},{1,0},{2,3},{3,2},{4,5},{5,4},{6,7},{7,6},{8,9},{9,8},{10,11... | collective-permute-start | bytes 331784 | tf_op jit(solution)/shard_map/ppermute | solution.py:1085
